TPU v7x, 32 devices: a whole 2x2x4 slice. The times are simulated.
32 devices in a mesh: groups: 2 (over x), expert: 8 (over z, y), latent: 2 (over core).
Axes of the slice: x: 2, y: 2, z: 4, core: 2. Of those that a mesh axis runs over, the one named last changes fastest.
Arguments:
- tokens: bfloat16 [8192, 4096], P(('groups', 'expert', 'latent')), parts along dimension 0, may hold values from -6 to 6
- routes: int32 [8192, 1], P(('groups', 'expert', 'latent')), parts along dimension 0, may hold values from 0 to 63; in each aligned block of 256 rows (0 to 255, 256 to 511, ...) at most 8 rows name the same one
- encoder: bfloat16 [128, 32, 4096], P(('groups', 'expert', 'latent')), parts along dimension 0, may hold values from -0.09375 to 0.09375
- encoder_bias: float32 [128, 32], P(('groups', 'expert', 'latent')), parts along dimension 0, may hold values from -3 to 3
- decoder: bfloat16 [128, 32, 4096], P(('groups', 'expert', 'latent')), parts along dimension 0, may hold values from -1 to 1
- encoder_mean: float32 [128, 32, 4096], P(('groups', 'expert', 'latent')), parts along dimension 0, may hold values from -256 to 256
- encoder_second: float32 [128, 32, 4096], P(('groups', 'expert', 'latent')), parts along dimension 0, may hold values from 16384 to 1638400
- bias_mean: float32 [128, 32], P(('groups', 'expert', 'latent')), parts along dimension 0, may hold values from -256 to 256
- bias_second: float32 [128, 32], P(('groups', 'expert', 'latent')), parts along dimension 0, may hold values from 16384 to 1638400
- decoder_mean: float32 [128, 32, 4096], P(('groups', 'expert', 'latent')), parts along dimension 0, may hold values from -18 to 18
- decoder_second: float32 [128, 32, 4096], P(('groups', 'expert', 'latent')), parts along dimension 0, may hold values from 4 to 400
Outputs:
- new_encoder: bfloat16 [128, 32, 4096], P(('groups', 'expert', 'latent')), parts along dimension 0
- new_encoder_bias: float32 [128, 32], P(('groups', 'expert', 'latent')), parts along dimension 0
- new_decoder: bfloat16 [128, 32, 4096], P(('groups', 'expert', 'latent')), parts along dimension 0
- new_encoder_mean: float32 [128, 32, 4096], P(('groups', 'expert', 'latent')), parts along dimension 0
- new_encoder_second: float32 [128, 32, 4096], P(('groups', 'expert', 'latent')), parts along dimension 0
- new_bias_mean: float32 [128, 32], P(('groups', 'expert', 'latent')), parts along dimension 0
- new_bias_second: float32 [128, 32], P(('groups', 'expert', 'latent')), parts along dimension 0
- new_decoder_mean: float32 [128, 32, 4096], P(('groups', 'expert', 'latent')), parts along dimension 0
- new_decoder_second: float32 [128, 32, 4096], P(('groups', 'expert', 'latent')), parts along dimension 0
- reconstruction: bfloat16 [8192, 4096], P(('groups', 'expert', 'latent')), parts along dimension 0
There are 2 independent parts, one for each index of `groups`. A program takes and returns all parts, laid end to end along the dimension named above; each array names one. Nothing has to cross between parts.
Inputs may be any that keep to these rules, and one draw needn't show every extreme that they name: `routes`: among the 256 rows of one device (aligned blocks of 256 rows), no expert is named by more than 8 rows, a bound that some block reaches.
All inputs are finite; a program needn't handle non-finite values.
Results may differ from a plain program's by a relative error of at most 0.0049.
Values may be sent and summed in bfloat16 or wider, within the bound.
A program may use at most 128 MiB of HBM per device.

v0:
```python
import jax
import jax.numpy as jnp
from jax import lax
from jax.sharding import PartitionSpec as P

beta_first = 0.9
beta_second = 0.999
adam_eps = 1e-08
learn_rate = 0.001
sparsity = 4.0
step_count = 1000.0


def adam_update(param, grad, mean, second):
    mean_new = beta_first * mean + (1.0 - beta_first) * grad
    second_new = beta_second * second + (1.0 - beta_second) * grad * grad
    corr_first = 1.0 - beta_first**step_count
    corr_second = 1.0 - beta_second**step_count
    update = mean_new / corr_first / (jnp.sqrt(second_new / corr_second) + adam_eps)
    return (param.astype(jnp.float32) - learn_rate * update, mean_new, second_new)


def body(
    tokens,
    routes,
    encoder,
    encoder_bias,
    decoder,
    encoder_mean,
    encoder_second,
    bias_mean,
    bias_second,
    decoder_mean,
    decoder_second,
):
    n_outer = lax.axis_size("expert")
    n_inner = lax.axis_size("latent")
    n_peers = n_outer * n_inner
    local_experts = encoder.shape[0]
    experts_all = n_peers * local_experts
    tok_rows = tokens.shape[0]
    width = tokens.shape[1]
    capacity = 2 * tok_rows // experts_all
    token_route = routes[:, 0]
    picked = (token_route[:, None] == jnp.arange(experts_all, dtype=jnp.int32)[None, :]).astype(
        jnp.int32
    )
    earlier = jnp.cumsum(picked, axis=0) - picked
    place_rank = jnp.sum(earlier * picked, axis=1)
    slot_index = token_route * capacity + place_rank
    tok_counts = jnp.sum(picked, axis=0)
    packed = jnp.zeros((experts_all * capacity, width), tokens.dtype).at[slot_index].set(tokens)
    direct_rows = packed.reshape(n_peers, local_experts, capacity, width)
    direct_counts = tok_counts.reshape(n_peers, local_experts, 1)
    got_rows, got_counts = (
        lax.all_to_all(direct_rows, ("expert", "latent"), split_axis=0, concat_axis=0, tiled=True),
        lax.all_to_all(
            direct_counts, ("expert", "latent"), split_axis=0, concat_axis=0, tiled=True
        ),
    )
    slot_place = jnp.arange(capacity, dtype=jnp.int32)
    filled = slot_place[None, None, :] < got_counts
    filled_mask = jnp.transpose(filled, (1, 0, 2))[:, None, :, :]
    preact = (
        jnp.einsum("gesd,eld->elgs", got_rows, encoder, preferred_element_type=jnp.float32)
        + encoder_bias[:, :, None, None]
    )
    active_mask = (preact > 0.0) & filled_mask
    activity = jnp.where(active_mask, preact, 0.0).astype(jnp.bfloat16)
    rebuilt = jnp.einsum("elgs,eld->gesd", activity, decoder, preferred_element_type=jnp.float32)
    residue = (rebuilt - got_rows.astype(jnp.float32)).astype(jnp.bfloat16)
    outgoing = rebuilt.astype(jnp.bfloat16)
    back_rows = lax.all_to_all(
        outgoing, ("expert", "latent"), split_axis=0, concat_axis=0, tiled=True
    )
    reconstruction = back_rows.reshape(experts_all * capacity, width)[slot_index]
    grad_activity = (
        jnp.einsum("gesd,eld->elgs", residue, decoder, preferred_element_type=jnp.float32)
        + sparsity
    )
    grad_preact = jnp.where(active_mask, grad_activity, 0.0)
    grad_bias = jnp.sum(grad_preact, axis=(2, 3))
    grad_narrow = grad_preact.astype(jnp.bfloat16)
    grad_enc = jnp.einsum(
        "elgs,gesd->eld", grad_narrow, got_rows, preferred_element_type=jnp.float32
    )
    grad_dec = jnp.einsum("elgs,gesd->eld", activity, residue, preferred_element_type=jnp.float32)
    new_enc, enc_mean, enc_second = adam_update(encoder, grad_enc, encoder_mean, encoder_second)
    new_bias, new_bias_mean, new_bias_second = adam_update(
        encoder_bias, grad_bias, bias_mean, bias_second
    )
    new_dec, dec_mean, dec_second = adam_update(decoder, grad_dec, decoder_mean, decoder_second)
    return (
        new_enc.astype(jnp.bfloat16),
        new_bias,
        new_dec.astype(jnp.bfloat16),
        enc_mean,
        enc_second,
        new_bias_mean,
        new_bias_second,
        dec_mean,
        dec_second,
        reconstruction,
    )


def solution(mesh):
    in_specs = (
        P(("groups", "expert", "latent"), None),
        P(("groups", "expert", "latent"), None),
        P(("groups", "expert", "latent"), None, None),
        P(("groups", "expert", "latent"), None),
        P(("groups", "expert", "latent"), None, None),
        P(("groups", "expert", "latent"), None, None),
        P(("groups", "expert", "latent"), None, None),
        P(("groups", "expert", "latent"), None),
        P(("groups", "expert", "latent"), None),
        P(("groups", "expert", "latent"), None, None),
        P(("groups", "expert", "latent"), None, None),
    )
    out_specs = (
        P(("groups", "expert", "latent"), None, None),
        P(("groups", "expert", "latent"), None),
        P(("groups", "expert", "latent"), None, None),
        P(("groups", "expert", "latent"), None, None),
        P(("groups", "expert", "latent"), None, None),
        P(("groups", "expert", "latent"), None),
        P(("groups", "expert", "latent"), None),
        P(("groups", "expert", "latent"), None, None),
        P(("groups", "expert", "latent"), None, None),
        P(("groups", "expert", "latent"), None),
    )
    return jax.shard_map(body, mesh=mesh, in_specs=in_specs, out_specs=out_specs, check_vma=False)
```

profile of v0, /device:TPU:13, one launch (start us, length us, event | category | flops | bytes accessed | tf_op | source)
XLA Modules:
  0.0 232.2 jit_solution(812846583522743883)
XLA Ops:
  0.6 0.7 fusion.23
  1.3 0.6 reduce-window.6
  1.9 0.2 slice_reduce_fusion
  2.2 0.9 convert_reduce_fusion
  3.1 0.7 reshape.54
  3.8 6.6 %all-to-all-start.1 = ((s32[16,4,1]{1,2,0:T(1,128)}), s32[16,4,1]{1,2,0:T(1,128)S(1)}, u32[]{:S(2)}, u32[]{:S(2)}) async-start(s32[16,4,1]{1,2,0:T(1,128)} %bitcast.9), calls=%async_computation.1 | async-start | bytes 16384 | tf_op jit(solution)/shard_map/all_to_all | solution.py:57
  10.3 0.7 compare_select_fusion
  11.0 7.0 %scatter_custom_fusion = bf16[512,4096]{1,0:T(8,128)(2,1)} fusion(s32[256]{0:T(256)S(1)} %bitcast.69, bf16[256,4096]{1,0:T(8,128)(2,1)} %param.11, bf16[]{:T(256)} %constant.13.clone.1), kind=kCustom, calls=%fused_computation.18 | custom fusion | bytes 4194816 | tf_op jit(solution)/shard_map/scatter | solution.py:52
  18.0 0.0 all-to-all-done.1
  18.0 0.0 copy-start.3
  18.0 0.0 copy-start.8
  18.0 6.2 %all-to-all-start = ((bf16[16,4,8,4096]{3,2,1,0:T(8,128)(2,1)}), bf16[16,4,8,4096]{3,2,1,0:T(8,128)(2,1)}, u32[]{:S(2)}, u32[]{:S(2)}) async-start(bf16[16,4,8,4096]{3,2,1,0:T(8,128)(2,1)} %bitcast.64), calls=%async_computation | async-start | bytes 8388608 | tf_op jit(solution)/shard_map/all_to_all | solution.py:56
  24.2 0.1 copy.37
  24.3 0.1 iota_compare_fusion.2
  24.4 0.0 copy-start
  24.4 92.3 %all-to-all-done = bf16[16,4,8,4096]{3,2,1,0:T(8,128)(2,1)} async-done(((bf16[16,4,8,4096]{3,2,1,0:T(8,128)(2,1)}), bf16[16,4,8,4096]{3,2,1,0:T(8,128)(2,1)}, u32[]{:S(2)}, u32[]{:S(2)}) %all-to-all-start) | async-done | bytes 4194336 | tf_op jit(solution)/shard_map/all_to_all | solution.py:56
  116.7 0.0 copy-done.3
  116.7 0.0 copy-done.8
  116.7 3.4 %fusion.13 = f32[4,32,16,8]{1,3,2,0:T(8,128)S(1)} fusion(bf16[16,4,8,4096]{3,2,1,0:T(8,128)(2,1)} %all-to-all-done, bf16[4,32,4096]{2,1,0:T(8,128)(2,1)S(1)} %copy-done.8, f32[4,32]{1,0:T(4,128)S(1)} %copy-done.3), kind=kOutput, calls=%fused_computation.24 | convolution fusion | flops 134234112 | bytes 5308928 | tf_op jit(solution)/shard_map/gesd,eld->elgs/dot_general | solution.py:65
  120.1 0.0 copy-done
  120.1 4.5 %bitcast_convert_fusion = (bf16[16,4,8,4096]{3,2,0,1:T(8,128)(2,1)S(1)}, f32[4,16,8,4096]{3,2,1,0:T(8,128)}) fusion(bf16[4,32,4096]{2,1,0:T(8,128)(2,1)S(1)} %copy-done, f32[4,32,16,8]{1,3,2,0:T(8,128)S(1)} %fusion.13, pred[4,16,8]{2,1,0:T(8,128)(4,1)S(1)} %iota_compare_fusion.2), kind=kOutput, calls=%fused_computation.2 | convolution fusion | flops 136380416 | bytes 13697536 | tf_op jit(solution)/shard_map/elgs,eld->gesd/dot_general | solution.py:70
  124.6 2.2 copy.40
  126.9 4.9 %all-to-all-start.2 = ((bf16[16,4,8,4096]{3,2,1,0:T(8,128)(2,1)}), bf16[16,4,8,4096]{3,2,1,0:T(8,128)(2,1)}, u32[]{:S(2)}, u32[]{:S(2)}) async-start(bf16[16,4,8,4096]{3,2,1,0:T(8,128)(2,1)} %copy.40), calls=%async_computation.2 | async-start | bytes 8388608 | tf_op jit(solution)/shard_map/all_to_all | solution.py:73
  131.8 0.0 copy-start.4
  131.8 0.0 copy-start.5
  131.8 0.0 copy-start.6
  131.8 0.0 copy-start.7
  131.8 0.0 slice-start
  131.8 6.0 %fusion.32 = (f32[4,32]{1,0:T(4,128)S(1)}, bf16[4,32,16,8]{1,3,2,0:T(8,128)(2,1)S(1)}) fusion(bf16[4,32,4096]{2,1,0:T(8,128)(2,1)S(1)} %copy-done, f32[4,16,8,4096]{3,2,1,0:T(8,128)} %get-tuple-element.24, bf16[16,4,8,4096]{3,2,1,0:T(8,128)(2,1)} %all-to-all-done, pred[4,16,8]{2,1,0:T(8,128)(4,1)S(1)} %iota_compare_fusion.2, f32[4,32,16,8]{1,3,2,0:T(8,128)S(1)} %fusion.13), kind=kOutput, calls=%fused_computation.52 | convolution fusion | flops 140607360 | bytes 13730816 | tf_op jit(solution)/shard_map/gesd,eld->elgs/dot_general | solution.py:78
  137.8 0.0 copy-done.4
  137.8 0.0 copy-done.5
  137.8 0.6 multiply_subtract_fusion
  138.4 0.0 copy-done.6
  138.4 0.0 copy-done.7
  138.4 0.0 slice-start.1
  138.4 0.0 copy-start.1
  138.4 0.0 copy-start.2
  138.5 6.9 %subtract_convert_fusion.1 = (bf16[4,32,4096]{2,1,0:T(8,128)(2,1)}, f32[4,32,4096]{2,1,0:T(8,128)}, f32[4,32,4096]{2,1,0:T(8,128)}) fusion(bf16[4,32,4096]{2,1,0:T(8,128)(2,1)S(1)} %copy-done.8, f32[4,32,4096]{2,1,0:T(8,128)S(1)} %copy-done.6, f32[4,32,4096]{2,1,0:T(8,128)S(1)} %copy-done.7, bf16[16,4,8,4096]{3,2,1,0:T(8,128)(2,1)} %all-to-all-done, ...), kind=kOutput, calls=%fused_computation.16 | convolution fusion | flops 141557760 | bytes 14712832 | tf_op jit(solution)/shard_map/elgs,gesd->eld/dot_general | solution.py:84
  145.3 0.0 slice-done
  145.3 0.0 slice-done.1
  145.3 0.0 copy-done.1
  145.3 0.0 copy-done.2
  145.3 7.3 %subtract_convert_fusion = (bf16[4,32,4096]{2,1,0:T(8,128)(2,1)}, f32[4,32,4096]{2,1,0:T(8,128)}, f32[4,32,4096]{2,1,0:T(8,128)}) fusion(bf16[4,32,4096]{2,1,0:T(8,128)(2,1)S(1)} %copy-done, f32[4,32,4096]{2,1,0:T(8,128)S(1)} %copy-done.1, f32[4,32,4096]{2,1,0:T(8,128)S(1)} %copy-done.2, f32[4,16,8,4096]{3,2,1,0:T(8,128)S(1)} %bitcast.63, ...), kind=kOutput, calls=%fused_computation.14 | convolution fusion | flops 147914752 | bytes 23134720 | tf_op jit(solution)/shard_map/elgs,gesd->eld/dot_general | solution.py:87
  152.6 71.6 %all-to-all-done.2 = bf16[16,4,8,4096]{3,2,1,0:T(8,128)(2,1)} async-done(((bf16[16,4,8,4096]{3,2,1,0:T(8,128)(2,1)}), bf16[16,4,8,4096]{3,2,1,0:T(8,128)(2,1)}, u32[]{:S(2)}, u32[]{:S(2)}) %all-to-all-start.2) | async-done | bytes 4194336 | tf_op jit(solution)/shard_map/all_to_all | solution.py:73
  224.2 7.9 %gather_fusion = bf16[256,4096]{1,0:T(8,128)(2,1)} fusion(bf16[512,4096]{1,0:T(8,128)(2,1)} %bitcast.20, s32[1024]{0:T(1024)S(1)} %pad_clamp_fusion), kind=kCustom, calls=%fused_computation | custom fusion | bytes 4195328 | tf_op jit(solution)/shard_map/gather | solution.py:76
  (4 shorter events, 0.0 us)
Async XLA Ops:
  3.8 14.3 %all-to-all-start.1 = ((s32[16,4,1]{1,2,0:T(1,128)}), s32[16,4,1]{1,2,0:T(1,128)S(1)}, u32[]{:S(2)}, u32[]{:S(2)}) async-start(s32[16,4,1]{1,2,0:T(1,128)} %bitcast.9), calls=%async_computation.1 | async-start | bytes 16384 | tf_op jit(solution)/shard_map/all_to_all | solution.py:57
  18.0 98.6 %copy-start.3 = (f32[4,32]{1,0:T(4,128)S(1)}, f32[4,32]{1,0:T(4,128)}, u32[]{:S(2)}) copy-start(f32[4,32]{1,0:T(4,128)} %param.14) | copy-start | bytes 1540
  18.0 98.6 %copy-start.8 = (bf16[4,32,4096]{2,1,0:T(8,128)(2,1)S(1)}, bf16[4,32,4096]{2,1,0:T(8,128)(2,1)}, u32[]{:S(2)}) copy-start(bf16[4,32,4096]{2,1,0:T(8,128)(2,1)} %param.13) | copy-start | bytes 3145732
  18.0 98.6 %all-to-all-start = ((bf16[16,4,8,4096]{3,2,1,0:T(8,128)(2,1)}), bf16[16,4,8,4096]{3,2,1,0:T(8,128)(2,1)}, u32[]{:S(2)}, u32[]{:S(2)}) async-start(bf16[16,4,8,4096]{3,2,1,0:T(8,128)(2,1)} %bitcast.64), calls=%async_computation | async-start | bytes 8388608 | tf_op jit(solution)/shard_map/all_to_all | solution.py:56
  24.4 95.8 %copy-start = (bf16[4,32,4096]{2,1,0:T(8,128)(2,1)S(1)}, bf16[4,32,4096]{2,1,0:T(8,128)(2,1)}, u32[]{:S(2)}) copy-start(bf16[4,32,4096]{2,1,0:T(8,128)(2,1)} %param.15) | copy-start | bytes 3145732
  126.9 97.4 %all-to-all-start.2 = ((bf16[16,4,8,4096]{3,2,1,0:T(8,128)(2,1)}), bf16[16,4,8,4096]{3,2,1,0:T(8,128)(2,1)}, u32[]{:S(2)}, u32[]{:S(2)}) async-start(bf16[16,4,8,4096]{3,2,1,0:T(8,128)(2,1)} %copy.40), calls=%async_computation.2 | async-start | bytes 8388608 | tf_op jit(solution)/shard_map/all_to_all | solution.py:73
  131.8 6.0 %copy-start.4 = (f32[4,32]{1,0:T(4,128)S(1)}, f32[4,32]{1,0:T(4,128)}, u32[]{:S(2)}) copy-start(f32[4,32]{1,0:T(4,128)} %param.19) | copy-start | bytes 1540
  131.8 6.0 %copy-start.5 = (f32[4,32]{1,0:T(4,128)S(1)}, f32[4,32]{1,0:T(4,128)}, u32[]{:S(2)}) copy-start(f32[4,32]{1,0:T(4,128)} %param.18) | copy-start | bytes 1540
  131.8 6.6 %copy-start.6 = (f32[4,32,4096]{2,1,0:T(8,128)S(1)}, f32[4,32,4096]{2,1,0:T(8,128)}, u32[]{:S(2)}) copy-start(f32[4,32,4096]{2,1,0:T(8,128)} %param.17) | copy-start | bytes 6291460
  131.8 6.6 %copy-start.7 = (f32[4,32,4096]{2,1,0:T(8,128)S(1)}, f32[4,32,4096]{2,1,0:T(8,128)}, u32[]{:S(2)}) copy-start(f32[4,32,4096]{2,1,0:T(8,128)} %param.16) | copy-start | bytes 6291460
  131.8 13.5 %slice-start = ((s8[8388608]{0:T(1024)(128)(4,1)}), s8[4194304]{0:T(1024)(128)(4,1)S(1)}, s32[]{:S(2)}) async-start(s8[8388608]{0:T(1024)(128)(4,1)} %bitcast.62), calls=%async_computation.3 | async-start | bytes 8388608
  138.4 6.9 %slice-start.1 = ((s8[8388608]{0:T(1024)(128)(4,1)}), s8[4194304]{0:T(1024)(128)(4,1)S(1)}, s32[]{:S(2)}) async-start(s8[8388608]{0:T(1024)(128)(4,1)} %bitcast.62), calls=%async_computation.4 | async-start | bytes 8388608
  138.4 6.9 %copy-start.1 = (f32[4,32,4096]{2,1,0:T(8,128)S(1)}, f32[4,32,4096]{2,1,0:T(8,128)}, u32[]{:S(2)}) copy-start(f32[4,32,4096]{2,1,0:T(8,128)} %param.21) | copy-start | bytes 6291460
  138.4 6.9 %copy-start.2 = (f32[4,32,4096]{2,1,0:T(8,128)S(1)}, f32[4,32,4096]{2,1,0:T(8,128)}, u32[]{:S(2)}) copy-start(f32[4,32,4096]{2,1,0:T(8,128)} %param.20) | copy-start | bytes 6291460
where the time goes:
time: 233 us; the launch traced here: 232 us
  waiting for transfers between devices  164 us (70%)
  matrix products  28.1 us (12%)
  local copies, waits for them, and re-layouts  18.2 us (8%)
  starting transfers between devices  17.6 us (8%)
  other arithmetic  3.58 us (2%)
    all_to_all x1, waiting for transfers between devices, body(): lax.all_to_all(direct_rows, ('expert', 'latent'), split_axis=0, concat_ax...  92.3 us
    all_to_all x1, waiting for transfers between devices, body(): lax.all_to_all(outgoing, ('expert', 'latent'), split_axis=0, concat_axis=...  71.6 us
    gather x1, local copies, waits for them, and re-layouts, body(): back_rows.reshape(experts_all * capacity, width)[slot_index]  7.93 us
    dot_general x1, matrix products, body(): jnp.einsum('elgs,gesd->eld', activity, residue, preferred_element_type=jn...  7.31 us
    scatter x1, local copies, waits for them, and re-layouts, body(): jnp.zeros((experts_all * capacity, width), tokens.dtype).at[slot_index]  7.04 us
    dot_general x1, matrix products, body(): jnp.einsum('elgs,gesd->eld', grad_narrow, got_rows, preferred_element_typ...  6.86 us
    all_to_all x1, starting transfers between devices, body(): lax.all_to_all(direct_counts, ('expert', 'latent'), split_axis=0, concat_...  6.55 us
    all_to_all x1, starting transfers between devices, body(): lax.all_to_all(direct_rows, ('expert', 'latent'), split_axis=0, concat_ax...  6.15 us
  transfers between devices with their start and end apart: 3, of which 2 were waited for; matrix products, arithmetic and copies ran while one was open for 12% of the time, Pallas kernels for 0%

commit v1 on v0

v1 whole, which is shorter than its diff:
```python
import jax
import jax.numpy as jnp
from jax import lax
from jax.sharding import PartitionSpec as P

beta_first = 0.9
beta_second = 0.999
adam_eps = 1e-08
learn_rate = 0.001
sparsity = 4.0
step_count = 1000.0
empty_mark = 8.0
peer_axes = ("expert", "latent")


def adam_update(param, grad, mean, second):
    mean_new = beta_first * mean + (1.0 - beta_first) * grad
    second_new = beta_second * second + (1.0 - beta_second) * grad * grad
    corr_first = 1.0 - beta_first**step_count
    corr_second = 1.0 - beta_second**step_count
    update = mean_new / corr_first / (jnp.sqrt(second_new / corr_second) + adam_eps)
    return (param.astype(jnp.float32) - learn_rate * update, mean_new, second_new)


def dot(a, b, dims):
    return lax.dot_general(a, b, (dims, ((), ())), preferred_element_type=jnp.float32)


def body(
    tokens,
    routes,
    encoder,
    encoder_bias,
    decoder,
    encoder_mean,
    encoder_second,
    bias_mean,
    bias_second,
    decoder_mean,
    decoder_second,
):
    n_peers = lax.axis_size("expert") * lax.axis_size("latent")
    own, lat, width = encoder.shape
    experts_all = n_peers * own
    tok_rows = tokens.shape[0]
    capacity = 2 * tok_rows // experts_all
    slots = experts_all * capacity
    bf16, f32 = jnp.bfloat16, jnp.float32

    route = routes[:, 0]
    picked = route[:, None] == jnp.arange(experts_all, dtype=jnp.int32)[None, :]
    lower = jnp.arange(tok_rows)[:, None] > jnp.arange(tok_rows)[None, :]
    earlier = dot(lower.astype(bf16), picked.astype(bf16), ((1,), (0,)))
    rank = jnp.sum(jnp.where(picked, earlier, 0.0), axis=1).astype(jnp.int32)
    slot = route * capacity + rank
    place = jnp.arange(slots, dtype=jnp.int32)[:, None] == slot[None, :]
    place_bf = place.astype(bf16)
    vacant = ~jnp.any(place, axis=1)
    mark = jnp.where(
        vacant[:, None] & (jnp.arange(width)[None, :] == 0), empty_mark, 0.0
    )
    packed = (dot(place_bf, tokens, ((1,), (0,))) + mark).astype(bf16)
    rows = lax.all_to_all(
        packed.reshape(n_peers, own * capacity, width), peer_axes, 0, 0, tiled=True
    ).reshape(slots, width)

    valid = rows[:, 0:1] < empty_mark - 1.0
    row_expert = (jnp.arange(slots, dtype=jnp.int32) // capacity) % own
    latent_expert = jnp.arange(own * lat, dtype=jnp.int32) // lat
    allowed = (row_expert[:, None] == latent_expert[None, :]) & valid
    enc = encoder.reshape(own * lat, width)
    dec = decoder.reshape(own * lat, width)
    preact = dot(rows, enc, ((1,), (1,))) + encoder_bias.reshape(1, own * lat)
    active = (preact > 0.0) & allowed
    activity = jnp.where(active, preact, 0.0).astype(bf16)
    rebuilt = dot(activity, dec, ((1,), (0,)))
    outgoing = rebuilt.astype(bf16)
    back = lax.all_to_all(
        outgoing.reshape(n_peers, own * capacity, width), peer_axes, 0, 0, tiled=True
    ).reshape(slots, width)
    residue = (rebuilt - rows.astype(f32)).astype(bf16)
    grad_activity = dot(residue, dec, ((1,), (1,))) + sparsity
    grad_preact = jnp.where(active, grad_activity, 0.0)
    grad_bias = jnp.sum(grad_preact, axis=0).reshape(own, lat)
    grad_enc = dot(grad_preact.astype(bf16), rows, ((0,), (0,))).reshape(own, lat, width)
    grad_dec = dot(activity, residue, ((0,), (0,))).reshape(own, lat, width)
    new_enc, enc_mean, enc_second = adam_update(encoder, grad_enc, encoder_mean, encoder_second)
    new_bias, new_bias_mean, new_bias_second = adam_update(
        encoder_bias, grad_bias, bias_mean, bias_second
    )
    new_dec, dec_mean, dec_second = adam_update(decoder, grad_dec, decoder_mean, decoder_second)

    reconstruction = dot(place_bf, back, ((0,), (0,))).astype(bf16)
    return (
        new_enc.astype(bf16),
        new_bias,
        new_dec.astype(bf16),
        enc_mean,
        enc_second,
        new_bias_mean,
        new_bias_second,
        dec_mean,
        dec_second,
        reconstruction,
    )


def solution(mesh):
    rows = P(("groups", "expert", "latent"), None)
    cubes = P(("groups", "expert", "latent"), None, None)
    in_specs = (rows, rows, cubes, rows, cubes, cubes, cubes, rows, rows, cubes, cubes)
    out_specs = (cubes, rows, cubes, cubes, cubes, rows, rows, cubes, cubes, rows)
    return jax.shard_map(body, mesh=mesh, in_specs=in_specs, out_specs=out_specs, check_vma=False)
```

time: 233 us -> 220 us (0.944)
  local copies, waits for them, and re-layouts: 18.2 us -> 2.11 us
  starting transfers between devices: 17.6 us -> 11.6 us
  matrix products: 28.1 us -> 33.9 us
  other arithmetic: 3.58 us -> 7.32 us
    gather x1 -> x0, local copies, waits for them, and re-layouts: 7.93 us -> none  [body(): back_rows.reshape(experts_all * capacity, width)[slot_index]]
    scatter x1 -> x0, local copies, waits for them, and re-layouts: 7.04 us -> none  [body(): jnp.zeros((experts_all * capacity, width), tokens.dtype).at[slot_index]]
    all_to_all x3 -> x2, starting transfers between devices: 17.6 us -> 11.6 us  [the longest x1 6.69 us: body(): lax.all_to_all(packed.reshape(n_peers, own * capacity, width), peer_axes,...]
    dot_general x5 -> x8, matrix products: 28.1 us -> 33.9 us  [dot(): lax.dot_general(a, b, (dims, ((), ())), preferred_element_type=jnp.float32)]
    convert_element_type x1, other arithmetic: 0.69 us -> 3.36 us  [body(): new_dec.astype(bf16)]
    all_to_all x3 -> x2, waiting for transfers between devices: 164 us -> 164 us  [the longest x1 92.4 us: body(): lax.all_to_all(packed.reshape(n_peers, own * capacity, width), peer_axes,...]
  transfers between devices with their start and end apart: 3 -> 2, of which waited for: 2 -> 2; matrix products, arithmetic and copies ran while one was open for 12% -> 9% of each run, Pallas kernels for 0% -> 0%
where the time goes in v1:
time: 220 us; the launch traced here: 219 us
  waiting for transfers between devices  164 us (75%)
  matrix products  33.9 us (15%)
  starting transfers between devices  11.6 us (5%)
  other arithmetic  7.32 us (3%)
    all_to_all x1, waiting for transfers between devices, body(): lax.all_to_all(packed.reshape(n_peers, own * capacity, width), peer_axes,...  92.4 us
    all_to_all x1, waiting for transfers between devices, body(): lax.all_to_all(outgoing.reshape(n_peers, own * capacity, width), peer_axe...  71.3 us
    dot_general x8, matrix products, dot(): lax.dot_general(a, b, (dims, ((), ())), preferred_element_type=jnp.float32)  33.9 us
    all_to_all x1, starting transfers between devices, body(): lax.all_to_all(packed.reshape(n_peers, own * capacity, width), peer_axes,...  6.69 us
    all_to_all x1, starting transfers between devices, body(): lax.all_to_all(outgoing.reshape(n_peers, own * capacity, width), peer_axe...  4.91 us
  transfers between devices with their start and end apart: 2, of which 2 were waited for; matrix products, arithmetic and copies ran while one was open for 9% of the time, Pallas kernels for 0%

profile of v1, /device:TPU:13, one launch (start us, length us, event | category | flops | bytes accessed | tf_op | source)
XLA Modules:
  0.0 219.4 jit_solution(11129556688313244506)
XLA Ops:
  0.6 0.0 copy-start
  0.7 1.0 fusion.2
  1.7 0.7 convert_add_fusion
  2.4 0.0 copy-start.6
  2.4 0.2 fusion.3
  2.6 0.0 copy-done
  2.6 3.5 %add_convert_fusion = bf16[512,4096]{1,0:T(8,128)(2,1)} fusion(bf16[256,4096]{1,0:T(8,128)(2,1)S(1)} %copy-done, pred[4096]{0:T(1024)(128)(4,1)S(1)} %iota_compare_fusion.7, pred[512]{0:T(512)(128)(4,1)S(1)} %not.7, s32[256]{0:T(256)S(1)} %convert_add_fusion), kind=kOutput, calls=%fused_computation.1 | convolution fusion | flops 1082261504 | bytes 6297088 | tf_op jit(solution)/shard_map/dot_general | solution.py:26
  6.1 0.0 copy-done.6
  6.1 0.0 copy-start.5
  6.1 6.7 %all-to-all-start = ((bf16[16,32,4096]{2,1,0:T(8,128)(2,1)}), bf16[16,32,4096]{2,1,0:T(8,128)(2,1)}, u32[]{:S(2)}, u32[]{:S(2)}) async-start(bf16[16,32,4096]{2,1,0:T(8,128)(2,1)} %bitcast.34), calls=%async_computation | async-start | bytes 8388608 | tf_op jit(solution)/shard_map/all_to_all | solution.py:63
  12.8 0.0 copy-done.5
  12.8 0.1 add.86
  12.9 92.4 %all-to-all-done = bf16[16,32,4096]{2,1,0:T(8,128)(2,1)} async-done(((bf16[16,32,4096]{2,1,0:T(8,128)(2,1)}), bf16[16,32,4096]{2,1,0:T(8,128)(2,1)}, u32[]{:S(2)}, u32[]{:S(2)}) %all-to-all-start) | async-done | bytes 4194336 | tf_op jit(solution)/shard_map/all_to_all | solution.py:63
  105.3 1.1 compare_reduce_fusion
  106.3 0.0 copy-start.1
  106.3 4.1 %convolution_add_fusion.1 = f32[512,128]{0,1:T(8,128)S(1)} fusion(bf16[512,4096]{1,0:T(8,128)(2,1)} %bitcast.2, bf16[128,4096]{1,0:T(8,128)(2,1)} %bitcast.35, f32[128]{0:T(128)S(1)} %add.86), kind=kOutput, calls=%fused_computation.12 | convolution fusion | flops 536936448 | bytes 5505536 | tf_op jit(solution)/shard_map/dot_general | solution.py:26
  110.4 0.0 copy-done.1
  110.5 6.8 %fusion.20 = (bf16[512,4096]{1,0:T(8,128)(2,1)}, bf16[512,4096]{1,0:T(8,128)(2,1)}) fusion(bf16[16,32,4096]{2,1,0:T(8,128)(2,1)} %all-to-all-done, bf16[128,4096]{1,0:T(8,128)(2,1)S(1)} %bitcast.31, f32[512,128]{0,1:T(8,128)S(1)} %convolution_add_fusion.1, pred[512]{0:T(512)(128)(4,1)S(1)} %compare_reduce_fusion, s32[128]{0:T(128)S(1)} %and_select_fusion, ...), kind=kOutput, calls=%fused_computation.56 | convolution fusion | flops 545652736 | bytes 13896704 | tf_op jit(solution)/shard_map/dot_general | solution.py:26
  117.2 4.9 %all-to-all-start.1 = ((bf16[16,32,4096]{2,1,0:T(8,128)(2,1)}), bf16[16,32,4096]{2,1,0:T(8,128)(2,1)}, u32[]{:S(2)}, u32[]{:S(2)}) async-start(bf16[16,32,4096]{2,1,0:T(8,128)(2,1)} %bitcast.30), calls=%async_computation.1 | async-start | bytes 8388608 | tf_op jit(solution)/shard_map/all_to_all | solution.py:78
  122.1 3.7 %fusion.4 = (bf16[128,512]{1,0:T(8,128)(2,1)S(1)}, f32[512,128]{0,1:T(8,128)S(1)}) fusion(s32[512]{0:T(512)S(1)} %add_select_fusion, s32[128]{0:T(128)S(1)} %and_select_fusion, pred[512]{0:T(512)(128)(4,1)S(1)} %compare_reduce_fusion, f32[512,128]{0,1:T(8,128)S(1)} %convolution_add_fusion.1, bf16[512,4096]{1,0:T(8,128)(2,1)} %get-tuple-element.20, ...), kind=kOutput, calls=%fused_computation.18 | convolution fusion | flops 537264128 | bytes 5901312 | tf_op jit(solution)/shard_map/dot_general | solution.py:26
  125.9 0.7 select_reduce_fusion
  126.6 1.3 reshape.106
  127.9 1.3 multiply_subtract_fusion
  129.2 0.0 copy-start.4
  129.2 0.0 copy-start.8
  129.2 0.0 copy-start.9
  129.2 3.1 %fusion.8 = f32[128,4096]{1,0:T(8,128)S(1)} fusion(bf16[512,4096]{1,0:T(8,128)(2,1)} %get-tuple-element.20, f32[512,128]{0,1:T(8,128)S(1)} %convolution_add_fusion.1, s32[512]{0:T(512)S(1)} %add_select_fusion, s32[128]{0:T(128)S(1)} %and_select_fusion, pred[512]{0:T(512)(128)(4,1)S(1)} %compare_reduce_fusion), kind=kOutput, calls=%fused_computation.30 | convolution fusion | flops 537264128 | bytes 6556672 | tf_op jit(solution)/shard_map/dot_general | solution.py:26
  132.4 0.0 copy-done.4
  132.4 0.0 copy-done.8
  132.4 0.6 copy-done.9
  133.0 0.0 copy-start.2
  133.0 0.0 copy-start.3
  133.0 6.9 %subtract_convert_fusion.2 = (bf16[4,32,4096]{2,1,0:T(8,128)(2,1)}, f32[4,32,4096]{2,1,0:T(8,128)}, f32[4,32,4096]{2,1,0:T(8,128)}) fusion(bf16[4,32,4096]{2,1,0:T(8,128)(2,1)S(1)} %copy-done.4, f32[4,32,4096]{2,1,0:T(8,128)S(1)} %copy-done.8, f32[4,32,4096]{2,1,0:T(8,128)S(1)} %copy-done.9, bf16[4,32,512]{2,1,0:T(8,128)(2,1)S(1)} %bitcast.36, ...), kind=kOutput, calls=%fused_computation.9 | convolution fusion | flops 544210944 | bytes 14811136 | tf_op jit(solution)/shard_map/dot_general | solution.py:26
  139.9 0.0 copy-done.2
  139.9 0.0 copy-done.3
  139.9 0.0 copy-start.7
  139.9 3.4 %subtract_convert_fusion.1 = (bf16[4,32,4096]{2,1,0:T(8,128)(2,1)}, f32[4,32,4096]{2,1,0:T(8,128)}, f32[4,32,4096]{2,1,0:T(8,128)}) fusion(bf16[4,32,4096]{2,1,0:T(8,128)(2,1)S(1)} %copy-done.1, f32[4,32,4096]{2,1,0:T(8,128)S(1)} %bitcast.33, f32[4,32,4096]{2,1,0:T(8,128)S(1)} %copy-done.2, f32[4,32,4096]{2,1,0:T(8,128)S(1)} %copy-done.3), kind=kLoop, calls=%fused_computation.7 | loop fusion | flops 7340032 | bytes 12582912 | tf_op jit(solution)/shard_map/convert_element_type | solution.py:97
  143.3 71.3 %all-to-all-done.1 = bf16[16,32,4096]{2,1,0:T(8,128)(2,1)} async-done(((bf16[16,32,4096]{2,1,0:T(8,128)(2,1)}), bf16[16,32,4096]{2,1,0:T(8,128)(2,1)}, u32[]{:S(2)}, u32[]{:S(2)}) %all-to-all-start.1) | async-done | bytes 4194336 | tf_op jit(solution)/shard_map/all_to_all | solution.py:78
  214.6 0.0 copy-done.7
  214.6 4.8 %convolution_convert_fusion = bf16[256,4096]{1,0:T(8,128)(2,1)} fusion(bf16[512,4096]{1,0:T(8,128)(2,1)} %bitcast.11, s32[256]{0:T(256)S(1)} %copy-done.7), kind=kOutput, calls=%fused_computation.2 | convolution fusion | flops 1074921472 | bytes 6292480 | tf_op jit(solution)/shard_map/dot_general | solution.py:26
  (4 shorter events, 0.0 us)
Async XLA Ops:
  0.6 1.9 copy-start
  2.4 3.7 %copy-start.6 = (s32[256]{0:T(256)}, s32[256]{0:T(256)S(1)}, u32[]{:S(2)}) copy-start(s32[256]{0:T(256)S(1)} %convert_add_fusion) | copy-start | bytes 3076
  6.1 6.7 %copy-start.5 = (f32[4,32]{1,0:T(4,128)S(1)}, f32[4,32]{1,0:T(4,128)}, u32[]{:S(2)}) copy-start(f32[4,32]{1,0:T(4,128)} %param.14) | copy-start | bytes 1540
  6.1 99.2 %all-to-all-start = ((bf16[16,32,4096]{2,1,0:T(8,128)(2,1)}), bf16[16,32,4096]{2,1,0:T(8,128)(2,1)}, u32[]{:S(2)}, u32[]{:S(2)}) async-start(bf16[16,32,4096]{2,1,0:T(8,128)(2,1)} %bitcast.34), calls=%async_computation | async-start | bytes 8388608 | tf_op jit(solution)/shard_map/all_to_all | solution.py:63
  106.3 4.1 %copy-start.1 = (bf16[4,32,4096]{2,1,0:T(8,128)(2,1)S(1)}, bf16[4,32,4096]{2,1,0:T(8,128)(2,1)}, u32[]{:S(2)}) copy-start(bf16[4,32,4096]{2,1,0:T(8,128)(2,1)} %param.15) | copy-start | bytes 3145732
  117.2 97.4 %all-to-all-start.1 = ((bf16[16,32,4096]{2,1,0:T(8,128)(2,1)}), bf16[16,32,4096]{2,1,0:T(8,128)(2,1)}, u32[]{:S(2)}, u32[]{:S(2)}) async-start(bf16[16,32,4096]{2,1,0:T(8,128)(2,1)} %bitcast.30), calls=%async_computation.1 | async-start | bytes 8388608 | tf_op jit(solution)/shard_map/all_to_all | solution.py:78
  129.2 3.1 %copy-start.4 = (bf16[4,32,4096]{2,1,0:T(8,128)(2,1)S(1)}, bf16[4,32,4096]{2,1,0:T(8,128)(2,1)}, u32[]{:S(2)}) copy-start(bf16[4,32,4096]{2,1,0:T(8,128)(2,1)} %param.13) | copy-start | bytes 3145732
  129.2 3.2 %copy-start.8 = (f32[4,32,4096]{2,1,0:T(8,128)S(1)}, f32[4,32,4096]{2,1,0:T(8,128)}, u32[]{:S(2)}) copy-start(f32[4,32,4096]{2,1,0:T(8,128)} %param.17) | copy-start | bytes 6291460
  129.2 3.8 %copy-start.9 = (f32[4,32,4096]{2,1,0:T(8,128)S(1)}, f32[4,32,4096]{2,1,0:T(8,128)}, u32[]{:S(2)}) copy-start(f32[4,32,4096]{2,1,0:T(8,128)} %param.16) | copy-start | bytes 6291460
  133.0 6.9 %copy-start.2 = (f32[4,32,4096]{2,1,0:T(8,128)S(1)}, f32[4,32,4096]{2,1,0:T(8,128)}, u32[]{:S(2)}) copy-start(f32[4,32,4096]{2,1,0:T(8,128)} %param.21) | copy-start | bytes 6291460
  133.0 6.9 %copy-start.3 = (f32[4,32,4096]{2,1,0:T(8,128)S(1)}, f32[4,32,4096]{2,1,0:T(8,128)}, u32[]{:S(2)}) copy-start(f32[4,32,4096]{2,1,0:T(8,128)} %param.20) | copy-start | bytes 6291460
  139.9 74.7 %copy-start.7 = (s32[256]{0:T(256)S(1)}, s32[256]{0:T(256)}, u32[]{:S(2)}) copy-start(s32[256]{0:T(256)} %copy-done.6) | copy-start | bytes 3076

commit v2 on v1

v2 whole, which is shorter than its diff:
```python
import jax
import jax.numpy as jnp
from jax import lax
from jax.sharding import PartitionSpec as P

beta_first = 0.9
beta_second = 0.999
adam_eps = 1e-08
learn_rate = 0.001
sparsity = 4.0
step_count = 1000.0
peer_axes = ("expert", "latent")


def adam_update(param, grad, mean, second):
    mean_new = beta_first * mean + (1.0 - beta_first) * grad
    second_new = beta_second * second + (1.0 - beta_second) * grad * grad
    corr_first = 1.0 - beta_first**step_count
    corr_second = 1.0 - beta_second**step_count
    update = mean_new / corr_first / (jnp.sqrt(second_new / corr_second) + adam_eps)
    return (param.astype(jnp.float32) - learn_rate * update, mean_new, second_new)


def dot(a, b, dims):
    return lax.dot_general(a, b, (dims, ((), ())), preferred_element_type=jnp.float32)


def body(
    tokens,
    routes,
    encoder,
    encoder_bias,
    decoder,
    encoder_mean,
    encoder_second,
    bias_mean,
    bias_second,
    decoder_mean,
    decoder_second,
):
    all_axes = ("groups",) + peer_axes
    n_groups, n_cores = lax.axis_size("groups"), lax.axis_size("latent")
    n_peers = lax.axis_size("expert") * n_cores
    n_chips = n_peers // n_cores
    own, lat, width = encoder.shape
    tok_rows = tokens.shape[0]
    chip_experts = n_cores * own
    half = own * lat
    block_full = 2 * tok_rows // n_peers
    block_small = 3 * block_full // 4
    bf16, f32, i32 = jnp.bfloat16, jnp.float32, jnp.int32
    core = lax.axis_index("latent")
    chip = lax.axis_index("expert")
    swap = [(i, n_cores - 1 - i) for i in range(n_cores)]

    route = routes[:, 0]
    everyone = lax.all_to_all(
        jnp.broadcast_to(route[None, :], (n_groups * n_peers, tok_rows)),
        all_axes,
        0,
        0,
        tiled=True,
    )
    enc_mine, dec_mine = encoder.reshape(half, width), decoder.reshape(half, width)
    enc_other = lax.ppermute(enc_mine, "latent", swap)
    dec_other = lax.ppermute(dec_mine, "latent", swap)
    bias_mine = encoder_bias.reshape(1, half)
    bias_other = lax.ppermute(bias_mine, "latent", swap)

    order = jnp.arange(tok_rows, dtype=i32)
    before = (order[:, None] < order[None, :]).astype(bf16)
    loads = jnp.sum(
        (everyone[:, :, None] // chip_experts == jnp.arange(n_chips)).astype(i32), axis=1
    )
    fits = jnp.max(loads) <= n_cores * block_small

    to_chip = route[None, :] // chip_experts == jnp.arange(n_chips, dtype=i32)[:, None]
    turn = jnp.sum(
        jnp.where(to_chip, dot(to_chip.astype(bf16), before, ((1,), (0,))), 0.0), axis=0
    ).astype(i32)
    target = route // chip_experts * n_cores + turn % n_cores
    spot = turn // n_cores

    peers = lax.dynamic_slice_in_dim(
        everyone, lax.axis_index("groups") * n_peers, n_peers, axis=0
    )
    for_chip = peers // chip_experts == chip
    peer_turn = dot(for_chip.astype(bf16), before, ((1,), (0,))).astype(i32)
    for_me = for_chip & (peer_turn % n_cores == core)
    inside = peers % chip_experts
    local = (inside // own + n_cores - core) % n_cores * own + inside % own
    label = jnp.where(for_me, local + 1, 0)
    peer_spot = peer_turn // n_cores

    def step(block):
        slots = n_peers * block
        place = jnp.arange(slots, dtype=i32)[:, None] == (target * block + spot)[None, :]
        place = place.astype(bf16)
        packed = dot(place, tokens, ((1,), (0,))).astype(bf16)
        rows = lax.all_to_all(
            packed.reshape(n_peers, block, width), peer_axes, 0, 0, tiled=True
        ).reshape(slots, width)
        hit = peer_spot[:, None, :] == jnp.arange(block, dtype=i32)[None, :, None]
        row_label = jnp.sum(jnp.where(hit, label[:, None, :], 0), axis=2).reshape(slots, 1)
        ahead = jnp.arange(half, dtype=i32)[None, :] // lat + 1
        allow_mine, allow_other = row_label == ahead, row_label == ahead + own

        def encode(enc, bias, allowed):
            preact = dot(rows, enc, ((1,), (1,))) + bias
            active = (preact > 0.0) & allowed
            return active, jnp.where(active, preact, 0.0).astype(bf16)

        active_mine, act_mine = encode(enc_mine, bias_mine, allow_mine)
        active_other, act_other = encode(enc_other, bias_other, allow_other)
        rebuilt = dot(
            jnp.concatenate([act_mine, act_other], axis=1),
            jnp.concatenate([dec_mine, dec_other], axis=0),
            ((1,), (0,)),
        )
        outgoing = rebuilt.astype(bf16)
        back = lax.all_to_all(
            outgoing.reshape(n_peers, block, width), peer_axes, 0, 0, tiled=True
        ).reshape(slots, width)
        residue = (rebuilt - rows.astype(f32)).astype(bf16)

        def gradients(active, act, dec):
            grad_activity = dot(residue, dec, ((1,), (1,))) + sparsity
            grad_preact = jnp.where(active, grad_activity, 0.0)
            return (
                dot(grad_preact.astype(bf16), rows, ((0,), (0,))),
                dot(act, residue, ((0,), (0,))),
                jnp.sum(grad_preact, axis=0, keepdims=True),
            )

        away = gradients(active_other, act_other, dec_other)
        arrived = [lax.ppermute(g, "latent", swap) for g in away]
        here = gradients(active_mine, act_mine, dec_mine)
        grad_enc, grad_dec, grad_bias = [x + y for x, y in zip(here, arrived)]
        new_enc, enc_mean, enc_second = adam_update(
            encoder, grad_enc.reshape(encoder.shape), encoder_mean, encoder_second
        )
        new_bias, new_bias_mean, new_bias_second = adam_update(
            encoder_bias, grad_bias.reshape(own, lat), bias_mean, bias_second
        )
        new_dec, dec_mean, dec_second = adam_update(
            decoder, grad_dec.reshape(decoder.shape), decoder_mean, decoder_second
        )
        reconstruction = dot(place, back, ((0,), (0,))).astype(bf16)
        return (
            new_enc.astype(bf16),
            new_bias,
            new_dec.astype(bf16),
            enc_mean,
            enc_second,
            new_bias_mean,
            new_bias_second,
            dec_mean,
            dec_second,
            reconstruction,
        )

    return lax.cond(fits, lambda: step(block_small), lambda: step(block_full))


def solution(mesh):
    rows = P(("groups", "expert", "latent"), None)
    cubes = P(("groups", "expert", "latent"), None, None)
    in_specs = (rows, rows, cubes, rows, cubes, cubes, cubes, rows, rows, cubes, cubes)
    out_specs = (cubes, rows, cubes, cubes, cubes, rows, rows, cubes, cubes, rows)
    return jax.shard_map(body, mesh=mesh, in_specs=in_specs, out_specs=out_specs, check_vma=False)
```

time: 220 us -> 186 us (0.85)
  waiting for transfers between devices: 164 us -> 121 us
  starting transfers between devices: 11.6 us -> 18.8 us
  matrix products: 33.9 us -> 30.2 us
  local copies, waits for them, and re-layouts: 2.11 us -> 5.26 us
    all_to_all x2 -> x3, waiting for transfers between devices: 164 us -> 119 us  [the longest x1 69.4 us: step(): lax.all_to_all(packed.reshape(n_peers, block, width), peer_axes, 0, 0, ti...]
    all_to_all x2 -> x3, starting transfers between devices: 11.6 us -> 16.7 us  [the longest x1 6.04 us: step(): lax.all_to_all(packed.reshape(n_peers, block, width), peer_axes, 0, 0, ti...]
    dot_general x8 -> x13, matrix products: 33.9 us -> 30.2 us  [dot(): lax.dot_general(a, b, (dims, ((), ())), preferred_element_type=jnp.float32)]
    ppermute x0 -> x6, waiting for transfers between devices: none -> 2.41 us  [the longest x3 2.4 us: step(): arrived = [lax.ppermute(g, 'latent', swap) for g in away]]
    unnamed x20 -> x60, local copies, waits for them, and re-layouts: 0.71 us -> 2.99 us
    convert_element_type x1 -> x2, other arithmetic: 3.36 us -> 4.71 us  [the longest x1 4.71 us: step(): new_dec.astype(bf16)]
  transfers between devices with their start and end apart: 2 -> 9, of which waited for: 2 -> 4; matrix products, arithmetic and copies ran while one was open for 9% -> 13% of each run, Pallas kernels for 0% -> 0%
where the time goes in v2:
time: 186 us
  waiting for transfers between devices  121 us (65%)
  matrix products  30.2 us (16%)
  starting transfers between devices  18.8 us (10%)
  other arithmetic  7.8 us (4%)
  local copies, waits for them, and re-layouts  5.26 us (3%)
    all_to_all x1, waiting for transfers between devices, step(): lax.all_to_all(packed.reshape(n_peers, block, width), peer_axes, 0, 0, ti...  69.4 us
    all_to_all x1, waiting for transfers between devices, step(): lax.all_to_all(outgoing.reshape(n_peers, block, width), peer_axes, 0, 0,...  45.8 us
    dot_general x13, matrix products, dot(): lax.dot_general(a, b, (dims, ((), ())), preferred_element_type=jnp.float32)  30.2 us
    all_to_all x1, starting transfers between devices, step(): lax.all_to_all(packed.reshape(n_peers, block, width), peer_axes, 0, 0, ti...  6.04 us
    all_to_all x1, starting transfers between devices, body(): lax.all_to_all(jnp.broadcast_to(route[None, :], (n_groups * n_peers, tok_...  5.74 us
    all_to_all x1, starting transfers between devices, step(): lax.all_to_all(outgoing.reshape(n_peers, block, width), peer_axes, 0, 0,...  4.89 us
    convert_element_type x1, other arithmetic, step(): new_dec.astype(bf16)  4.71 us
  transfers between devices with their start and end apart: 9, of which 4 were waited for; matrix products, arithmetic and copies ran while one was open for 13% of the time, Pallas kernels for 0%

profile of v2, /device:TPU:13, one launch (start us, length us, event | category | flops | bytes accessed | tf_op | source)
XLA Modules:
  0.0 185.7 jit_solution(11249554042854145007)
XLA Ops:
  0.6 0.8 reshape.280
  1.4 0.7 collective-permute-start.7
  2.1 1.3 broadcast_in_dim.77
  3.4 5.7 %all-to-all-start.4 = ((s32[32,1,256]{2,1,0:T(1,128)}), s32[32,1,256]{2,1,0:T(1,128)S(1)}, u32[]{:S(2)}, u32[]{:S(2)}) async-start(s32[32,1,256]{2,1,0:T(1,128)} %broadcast_in_dim.77), calls=%async_computation.4 | async-start | bytes 65536 | tf_op jit(solution)/shard_map/all_to_all | solution.py:57
  9.1 0.4 collective-permute-start.6
  9.6 0.1 collective-permute-start.8
  9.7 0.7 and_select_fusion.6
  10.4 0.2 fusion.58
  10.6 3.6 %all-to-all-done.4 = s32[32,1,256]{2,1,0:T(1,128)S(1)} async-done(((s32[32,1,256]{2,1,0:T(1,128)}), s32[32,1,256]{2,1,0:T(1,128)S(1)}, u32[]{:S(2)}, u32[]{:S(2)}) %all-to-all-start.4) | async-done | bytes 32800 | tf_op jit(solution)/shard_map/all_to_all | solution.py:57
  14.2 0.2 fusion.69
  14.4 0.6 convert_reduce_fusion
  15.1 0.6 reduce_max.9
  16.5 167.4 %conditional.4 = (f32[4,32]{1,0:T(4,128)S(1)}, f32[4,32,4096]{2,1,0:T(8,128)}, f32[4,32,4096]{2,1,0:T(8,128)}, f32[4,32]{1,0:T(4,128)S(1)}, f32[4,32]{1,0:T(4,12...) conditional(s32[]{:T(128)} %convert_element_type.107, ...), branch_computations={%region_3.7_spmd, %region_7.11_spmd} | conditional | flops 7549611008 | bytes 211780848
  16.7 0.0 copy-start.43
  16.8 4.9 %convolution_convert_fusion.1 = bf16[384,4096]{1,0:T(8,128)(2,1)} fusion(bf16[256,4096]{1,0:T(8,128)(2,1)} %get-tuple-element.379, s32[256]{0:T(256)S(1)} %fusion.55), kind=kOutput, calls=%fused_computation.72 | convolution fusion | flops 806977536 | bytes 5243904 | tf_op jit(solution)/shard_map/cond/branch_1_fun/dot_general | solution.py:25
  21.7 6.0 %all-to-all-start.2 = ((bf16[16,24,4096]{2,1,0:T(8,128)(2,1)}), bf16[16,24,4096]{2,1,0:T(8,128)(2,1)S(1)}, u32[]{:S(2)}, u32[]{:S(2)}) async-start(bf16[16,24,4096]{2,1,0:T(8,128)(2,1)} %bitcast.116), calls=%async_computation.2 | async-start | bytes 6291456 | tf_op jit(solution)/shard_map/cond/branch_1_fun/all_to_all | solution.py:100
  27.8 0.3 select_reduce_fusion.1
  28.2 0.1 eq.92
  28.3 69.4 %all-to-all-done.2 = bf16[16,24,4096]{2,1,0:T(8,128)(2,1)S(1)} async-done(((bf16[16,24,4096]{2,1,0:T(8,128)(2,1)}), bf16[16,24,4096]{2,1,0:T(8,128)(2,1)S(1)}, u32[]{:S(2)}, u32[]{:S(2)}) %all-to-all-start.2) | async-done | bytes 3145760 | tf_op jit(solution)/shard_map/cond/branch_1_fun/all_to_all | solution.py:100
  97.7 2.3 %convolution_add_fusion.10 = f32[384,128]{1,0:T(8,128)S(1)} fusion(bf16[384,4096]{1,0:T(8,128)(2,1)S(1)} %bitcast.110, bf16[128,4096]{1,0:T(8,128)(2,1)} %copy-done.20, f32[128]{0:T(128)S(1)} %bitcast.135), kind=kOutput, calls=%fused_computation.91 | convolution fusion | flops 402702336 | bytes 4391424 | tf_op jit(solution)/shard_map/cond/branch_1_fun/dot_general | solution.py:25
  100.0 0.0 copy-start.18
  100.0 1.7 select_convert_fusion.3
  101.7 3.7 %fusion.81 = (bf16[384,4096]{1,0:T(8,128)(2,1)}, bf16[384,4096]{1,0:T(8,128)(2,1)}) fusion(bf16[16,24,4096]{2,1,0:T(8,128)(2,1)S(1)} %all-to-all-done.2, bf16[128,4096]{1,0:T(8,128)(2,1)S(1)} %copy-done.18, bf16[128,4096]{1,0:T(8,128)(2,1)S(1)} %bitcast.122, bf16[384,128]{1,0:T(8,128)(2,1)S(1)} %get-tuple-element.492, ...), kind=kOutput, calls=%fused_computation.197 | convolution fusion | flops 816185344 | bytes 11730944 | tf_op jit(solution)/shard_map/cond/branch_1_fun/dot_general | solution.py:25
  105.4 4.9 %all-to-all-start.3 = ((bf16[16,24,4096]{2,1,0:T(8,128)(2,1)}), bf16[16,24,4096]{2,1,0:T(8,128)(2,1)}, u32[]{:S(2)}, u32[]{:S(2)}) async-start(bf16[16,24,4096]{2,1,0:T(8,128)(2,1)} %bitcast.115), calls=%async_computation.3 | async-start | bytes 6291456 | tf_op jit(solution)/shard_map/cond/branch_1_fun/all_to_all | solution.py:121
  110.3 0.0 copy-start.19
  110.3 4.1 %fusion.85 = f32[128,4096]{1,0:T(8,128)} fusion(bf16[384,128]{1,0:T(8,128)(2,1)S(1)} %get-tuple-element.492, bf16[384,4096]{1,0:T(8,128)(2,1)} %get-tuple-element.490), kind=kOutput, calls=%fused_computation.201 | convolution fusion | flops 402653184 | bytes 5341184 | tf_op jit(solution)/shard_map/cond/branch_1_fun/dot_general | solution.py:25
  114.4 0.4 collective-permute-start.5
  114.8 1.0 fusion.82
  115.8 0.0 copy-start.46
  115.8 2.1 %fusion.43 = f32[128,4096]{1,0:T(8,128)} fusion(bf16[384,4096]{1,0:T(8,128)(2,1)S(1)} %bitcast.112, bf16[384,128]{1,0:T(8,128)(2,1)S(1)} %get-tuple-element.495), kind=kOutput, calls=%fused_computation.106 | convolution fusion | flops 402653184 | bytes 5341184 | tf_op jit(solution)/shard_map/cond/branch_1_fun/dot_general | solution.py:25
  117.9 0.2 collective-permute-start.4
  118.0 0.4 collective-permute-start.3
  118.4 0.0 copy-start.34
  118.4 1.0 fusion.83
  119.4 2.4 %collective-permute-done.3 = f32[1,128]{1,0:T(1,128)S(1)} collective-permute-done((f32[1,128]{1,0:T(1,128)S(1)}, f32[1,128]{1,0:T(1,128)S(1)}, u32[]{:S(2)}, u32[]{:S(2)}) %collective-permute-start.3) | collective-permute-done | bytes 544 | tf_op jit(solution)/shard_map/cond/branch_1_fun/ppermute | solution.py:136
  121.8 0.1 reshape.271
  121.9 0.6 multiply_subtract_fusion.1
  122.6 3.4 %convolution_add_fusion.6 = f32[128,4096]{1,0:T(8,128)S(1)} fusion(f32[128,4096]{1,0:T(8,128)} %collective-permute-done.5, bf16[384,128]{1,0:T(8,128)(2,1)S(1)} %get-tuple-element.491, bf16[384,4096]{1,0:T(8,128)(2,1)} %get-tuple-element.490), kind=kOutput, calls=%fused_computation.73 | convolution fusion | flops 403177472 | bytes 7438336 | tf_op jit(solution)/shard_map/cond/branch_1_fun/dot_general | solution.py:25
  126.0 0.0 copy-start.5
  126.0 0.0 copy-start.11
  126.0 2.5 %convolution_add_fusion.7 = f32[128,4096]{1,0:T(8,128)S(1)} fusion(f32[128,4096]{1,0:T(8,128)} %collective-permute-done.4, bf16[384,4096]{1,0:T(8,128)(2,1)S(1)} %bitcast.113, bf16[384,128]{1,0:T(8,128)(2,1)S(1)} %get-tuple-element.497), kind=kOutput, calls=%fused_computation.74 | convolution fusion | flops 403177472 | bytes 7438336 | tf_op jit(solution)/shard_map/cond/branch_1_fun/dot_general | solution.py:25
  128.6 0.6 copy-done.9
  129.2 0.6 copy-done.11
  129.8 4.7 %subtract_convert_fusion.4 = (bf16[4,32,4096]{2,1,0:T(8,128)(2,1)S(1)}, f32[4,32,4096]{2,1,0:T(8,128)}, f32[4,32,4096]{2,1,0:T(8,128)}, bf16[4,32,4096]{2,1,0:T(...) fusion(bf16[4,32,4096]{2,1,0:T(8,128)(2,1)S(1)} %copy-done.5, f32[4,32,4096]{2,1,0:T(8,128)S(1)} %bitcast.125, ...), kind=kLoop, calls=%fused_computation.83 | loop fusion | flops 14680064 | bytes 25165824 | tf_op jit(solution)/shard_map/cond/branch_0_fun/convert_element_type | solution.py:152
  134.5 45.8 %all-to-all-done.3 = bf16[16,24,4096]{2,1,0:T(8,128)(2,1)} async-done(((bf16[16,24,4096]{2,1,0:T(8,128)(2,1)}), bf16[16,24,4096]{2,1,0:T(8,128)(2,1)}, u32[]{:S(2)}, u32[]{:S(2)}) %all-to-all-start.3) | async-done | bytes 3145760 | tf_op jit(solution)/shard_map/cond/branch_1_fun/all_to_all | solution.py:121
  180.3 3.2 %fusion.37 = bf16[256,4096]{1,0:T(8,128)(2,1)S(1)} fusion(bf16[384,4096]{1,0:T(8,128)(2,1)} %bitcast.19, s32[256]{0:T(256)S(1)} %copy-done.26), kind=kOutput, calls=%fused_computation.96 | convolution fusion | flops 805404672 | bytes 5243904 | tf_op jit(solution)/shard_map/cond/branch_1_fun/dot_general | solution.py:25
  183.9 1.3 copy-done.21
  185.2 0.3 copy-done.22
  (76 shorter events, 0.3 us)
Async XLA Ops:
  1.4 15.0 %collective-permute-start.7 = (f32[1,128]{1,0:T(1,128)S(1)}, f32[1,128]{1,0:T(1,128)S(1)}, u32[]{:S(2)}, u32[]{:S(2)}) collective-permute-start(f32[1,128]{1,0:T(1,128)S(1)} %reshape.280), channel_id=1, source_target_pairs={{0,1},{1,0},{2,3},{3,2},{4,5},{5,4},{6,7},{7,6},{8,9},{9,8},{10,11... | collective-permute-start | bytes 1544 | tf_op jit(solution)/shard_map/ppermute | solution.py:68
  3.4 10.8 %all-to-all-start.4 = ((s32[32,1,256]{2,1,0:T(1,128)}), s32[32,1,256]{2,1,0:T(1,128)S(1)}, u32[]{:S(2)}, u32[]{:S(2)}) async-start(s32[32,1,256]{2,1,0:T(1,128)} %broadcast_in_dim.77), calls=%async_computation.4 | async-start | bytes 65536 | tf_op jit(solution)/shard_map/all_to_all | solution.py:57
  9.1 7.2 %collective-permute-start.6 = (bf16[128,4096]{1,0:T(8,128)(2,1)}, bf16[128,4096]{1,0:T(8,128)(2,1)S(1)}, u32[]{:S(2)}, u32[]{:S(2)}) collective-permute-start(bf16[128,4096]{1,0:T(8,128)(2,1)} %bitcast.129), channel_id=1, source_target_pairs={{0,1},{1,0},{2,3},{3,2},{4,5},{5,4},{6,7},{7,6},{8,9},{9,8},{10,11... | collective-permute-start | bytes 3145736 | tf_op jit(solution)/shard_map/ppermute | solution.py:65
  9.6 6.8 %collective-permute-start.8 = (bf16[128,4096]{1,0:T(8,128)(2,1)}, bf16[128,4096]{1,0:T(8,128)(2,1)S(1)}, u32[]{:S(2)}, u32[]{:S(2)}) collective-permute-start(bf16[128,4096]{1,0:T(8,128)(2,1)} %bitcast.117), channel_id=1, source_target_pairs={{0,1},{1,0},{2,3},{3,2},{4,5},{5,4},{6,7},{7,6},{8,9},{9,8},{10,11... | collective-permute-start | bytes 3145736 | tf_op jit(solution)/shard_map/ppermute | solution.py:66
  16.7 5.0 %copy-start.17 = (bf16[128,4096]{1,0:T(8,128)(2,1)}, bf16[128,4096]{1,0:T(8,128)(2,1)S(1)}, u32[]{:S(2)}) copy-start(bf16[128,4096]{1,0:T(8,128)(2,1)S(1)} %get-tuple-element.399) | copy-start | bytes 3145732
  16.7 5.0 %copy-start.20 = (bf16[128,4096]{1,0:T(8,128)(2,1)}, bf16[128,4096]{1,0:T(8,128)(2,1)S(1)}, u32[]{:S(2)}) copy-start(bf16[128,4096]{1,0:T(8,128)(2,1)S(1)} %get-tuple-element.396) | copy-start | bytes 3145732
  16.7 5.0 %copy-start.43 = (f32[1,128]{1,0:T(1,128)}, f32[1,128]{1,0:T(1,128)S(1)}, u32[]{:S(2)}) copy-start(f32[1,128]{1,0:T(1,128)S(1)} %get-tuple-element.381) | copy-start | bytes 1540
  16.8 4.9 %copy-start.25 = (s32[256]{0:T(256)}, s32[256]{0:T(256)S(1)}, u32[]{:S(2)}) copy-start(s32[256]{0:T(256)S(1)} %fusion.55) | copy-start | bytes 3076
  21.7 76.0 %all-to-all-start.2 = ((bf16[16,24,4096]{2,1,0:T(8,128)(2,1)}), bf16[16,24,4096]{2,1,0:T(8,128)(2,1)S(1)}, u32[]{:S(2)}, u32[]{:S(2)}) async-start(bf16[16,24,4096]{2,1,0:T(8,128)(2,1)} %bitcast.116), calls=%async_computation.2 | async-start | bytes 6291456 | tf_op jit(solution)/shard_map/cond/branch_1_fun/all_to_all | solution.py:100
  97.7 2.3 %copy-start.15 = (bf16[4,32,4096]{2,1,0:T(8,128)(2,1)S(1)}, bf16[4,32,4096]{2,1,0:T(8,128)(2,1)}, u32[]{:S(2)}) copy-start(bf16[4,32,4096]{2,1,0:T(8,128)(2,1)} %get-tuple-element.405) | copy-start | bytes 3145732
  97.7 2.3 %copy-start.44 = (f32[1,128]{1,0:T(1,128)S(1)}, f32[1,128]{1,0:T(1,128)}, u32[]{:S(2)}) copy-start(f32[1,128]{1,0:T(1,128)} %copy-done.43) | copy-start | bytes 1540
  100.0 1.7 copy-start.3
  100.0 1.7 copy-start.18
  105.4 74.9 %all-to-all-start.3 = ((bf16[16,24,4096]{2,1,0:T(8,128)(2,1)}), bf16[16,24,4096]{2,1,0:T(8,128)(2,1)}, u32[]{:S(2)}, u32[]{:S(2)}) async-start(bf16[16,24,4096]{2,1,0:T(8,128)(2,1)} %bitcast.115), calls=%async_computation.3 | async-start | bytes 6291456 | tf_op jit(solution)/shard_map/cond/branch_1_fun/all_to_all | solution.py:121
  110.3 4.5 %copy-start.1 = (bf16[384,4096]{1,0:T(8,128)(2,1)S(1)}, bf16[384,4096]{1,0:T(8,128)(2,1)}, u32[]{:S(2)}) copy-start(bf16[384,4096]{1,0:T(8,128)(2,1)} %get-tuple-element.490) | copy-start | bytes 9437188
  110.3 4.5 %copy-start.19 = (bf16[128,4096]{1,0:T(8,128)(2,1)S(1)}, bf16[128,4096]{1,0:T(8,128)(2,1)}, u32[]{:S(2)}) copy-start(bf16[128,4096]{1,0:T(8,128)(2,1)} %copy-done.17) | copy-start | bytes 3145732
  114.4 8.1 %collective-permute-start.5 = (f32[128,4096]{1,0:T(8,128)}, f32[128,4096]{1,0:T(8,128)}, u32[]{:S(2)}, u32[]{:S(2)}) collective-permute-start(f32[128,4096]{1,0:T(8,128)} %fusion.85), channel_id=1, source_target_pairs={{0,1},{1,0},{2,3},{3,2},{4,5},{5,4},{6,7},{7,6},{8,9},{9,8},{10,11... | collective-permute-start | bytes 6291464 | tf_op jit(solution)/shard_map/cond/branch_1_fun/ppermute | solution.py:136
  115.8 2.6 %copy-start.4 = (bf16[4,32,4096]{2,1,0:T(8,128)(2,1)S(1)}, bf16[4,32,4096]{2,1,0:T(8,128)(2,1)}, u32[]{:S(2)}) copy-start(bf16[4,32,4096]{2,1,0:T(8,128)(2,1)} %get-tuple-element.406) | copy-start | bytes 3145732
  115.8 2.6 %copy-start.46 = (f32[384,128]{1,0:T(8,128)S(1)}, f32[384,128]{1,0:T(8,128)}, u32[]{:S(2)}) copy-start(f32[384,128]{1,0:T(8,128)} %get-tuple-element.493) | copy-start | bytes 589828
  117.9 8.1 %collective-permute-start.4 = (f32[128,4096]{1,0:T(8,128)}, f32[128,4096]{1,0:T(8,128)}, u32[]{:S(2)}, u32[]{:S(2)}) collective-permute-start(f32[128,4096]{1,0:T(8,128)} %fusion.43), channel_id=1, source_target_pairs={{0,1},{1,0},{2,3},{3,2},{4,5},{5,4},{6,7},{7,6},{8,9},{9,8},{10,11... | collective-permute-start | bytes 6291464 | tf_op jit(solution)/shard_map/cond/branch_1_fun/ppermute | solution.py:136
  118.0 3.8 %collective-permute-start.3 = (f32[1,128]{1,0:T(1,128)S(1)}, f32[1,128]{1,0:T(1,128)S(1)}, u32[]{:S(2)}, u32[]{:S(2)}) collective-permute-start(f32[1,128]{1,0:T(1,128)S(1)} %bitcast.141), channel_id=1, source_target_pairs={{0,1},{1,0},{2,3},{3,2},{4,5},{5,4},{6,7},{7,6},{8,9},{9,8},{10,11... | collective-permute-start | bytes 1544 | tf_op jit(solution)/shard_map/cond/branch_1_fun/ppermute | solution.py:136
  118.4 3.5 %copy-start.28 = (f32[4,32]{1,0:T(4,128)S(1)}, f32[4,32]{1,0:T(4,128)}, u32[]{:S(2)}) copy-start(f32[4,32]{1,0:T(4,128)} %get-tuple-element.369) | copy-start | bytes 1540
  118.4 3.5 %copy-start.32 = (f32[4,32]{1,0:T(4,128)S(1)}, f32[4,32]{1,0:T(4,128)}, u32[]{:S(2)}) copy-start(f32[4,32]{1,0:T(4,128)} %get-tuple-element.370) | copy-start | bytes 1540
  118.4 3.5 %copy-start.34 = (f32[4,32]{1,0:T(4,128)S(1)}, f32[4,32]{1,0:T(4,128)}, u32[]{:S(2)}) copy-start(f32[4,32]{1,0:T(4,128)} %get-tuple-element.400) | copy-start | bytes 1540
  122.5 6.0 %copy-start.13 = (f32[4,32,4096]{2,1,0:T(8,128)S(1)}, f32[4,32,4096]{2,1,0:T(8,128)}, u32[]{:S(2)}) copy-start(f32[4,32,4096]{2,1,0:T(8,128)} %get-tuple-element.404) | copy-start | bytes 6291460
  122.5 6.0 %copy-start.16 = (bf16[4,32,4096]{2,1,0:T(8,128)(2,1)S(1)}, bf16[4,32,4096]{2,1,0:T(8,128)(2,1)}, u32[]{:S(2)}) copy-start(bf16[4,32,4096]{2,1,0:T(8,128)(2,1)} %get-tuple-element.405) | copy-start | bytes 3145732
  126.0 2.6 %copy-start.5 = (bf16[4,32,4096]{2,1,0:T(8,128)(2,1)S(1)}, bf16[4,32,4096]{2,1,0:T(8,128)(2,1)}, u32[]{:S(2)}) copy-start(bf16[4,32,4096]{2,1,0:T(8,128)(2,1)} %get-tuple-element.406) | copy-start | bytes 3145732
  126.0 2.6 %copy-start.7 = (f32[4,32,4096]{2,1,0:T(8,128)S(1)}, f32[4,32,4096]{2,1,0:T(8,128)}, u32[]{:S(2)}) copy-start(f32[4,32,4096]{2,1,0:T(8,128)} %get-tuple-element.401) | copy-start | bytes 6291460
  126.0 3.2 %copy-start.9 = (f32[4,32,4096]{2,1,0:T(8,128)S(1)}, f32[4,32,4096]{2,1,0:T(8,128)}, u32[]{:S(2)}) copy-start(f32[4,32,4096]{2,1,0:T(8,128)} %get-tuple-element.402) | copy-start | bytes 6291460
  126.0 3.8 %copy-start.11 = (f32[4,32,4096]{2,1,0:T(8,128)S(1)}, f32[4,32,4096]{2,1,0:T(8,128)}, u32[]{:S(2)}) copy-start(f32[4,32,4096]{2,1,0:T(8,128)} %get-tuple-element.403) | copy-start | bytes 6291460
  129.8 50.5 %copy-start.26 = (s32[256]{0:T(256)S(1)}, s32[256]{0:T(256)}, u32[]{:S(2)}) copy-start(s32[256]{0:T(256)} %copy-done.25) | copy-start | bytes 3076
  180.3 3.2 %copy-start.35 = (f32[4,32]{1,0:T(4,128)S(1)}, f32[4,32]{1,0:T(4,128)}, u32[]{:S(2)}) copy-start(f32[4,32]{1,0:T(4,128)} %get-tuple-element.525) | copy-start | bytes 1540
  180.3 3.3 %copy-start.37 = (f32[4,32]{1,0:T(4,128)S(1)}, f32[4,32]{1,0:T(4,128)}, u32[]{:S(2)}) copy-start(f32[4,32]{1,0:T(4,128)} %get-tuple-element.529) | copy-start | bytes 1540
  180.3 3.3 %copy-start.39 = (f32[4,32]{1,0:T(4,128)S(1)}, f32[4,32]{1,0:T(4,128)}, u32[]{:S(2)}) copy-start(f32[4,32]{1,0:T(4,128)} %get-tuple-element.528) | copy-start | bytes 1540
  183.9 1.3 copy-start.21
  183.9 1.6 copy-start.22
  183.9 1.6 copy-start.36
  183.9 1.6 copy-start.38
  183.9 1.6 copy-start.40

commit v3 on v2

--- a/solution.py
+++ b/solution.py
@@ -92,11 +92,14 @@
     label = jnp.where(for_me, local + 1, 0)
     peer_spot = peer_turn // n_cores
 
-    def step(block):
+    def pack(block):
+        at = jnp.where(spot < block, target * block + spot, -1)
+        place = jnp.arange(n_peers * block, dtype=i32)[:, None] == at[None, :]
+        place = place.astype(bf16)
+        return place, dot(place, tokens, ((1,), (0,))).astype(bf16)
+
+    def step(block, place, packed):
         slots = n_peers * block
-        place = jnp.arange(slots, dtype=i32)[:, None] == (target * block + spot)[None, :]
-        place = place.astype(bf16)
-        packed = dot(place, tokens, ((1,), (0,))).astype(bf16)
         rows = lax.all_to_all(
             packed.reshape(n_peers, block, width), peer_axes, 0, 0, tiled=True
         ).reshape(slots, width)
@@ -159,7 +162,10 @@
             reconstruction,
         )
 
-    return lax.cond(fits, lambda: step(block_small), lambda: step(block_full))
+    early = pack(block_small)
+    return lax.cond(
+        fits, lambda: step(block_small, *early), lambda: step(block_full, *pack(block_full))
+    )
 
 
 def solution(mesh):

time: 186 us -> 186 us (level)
  waiting for transfers between devices: 121 us -> 117 us
  local copies, waits for them, and re-layouts: 5.26 us -> 9.03 us
    sub x1 -> x2, other arithmetic: 0.6 us -> 5.31 us  [adam_update(): param.astype(jnp.float32) - learn_rate * update]
    convert_element_type x1, other arithmetic: 4.71 us -> 0.73 us  [pack(): place = place.astype(bf16)]
    unnamed x60 -> x65, local copies, waits for them, and re-layouts: 2.99 us -> 6.77 us
    all_to_all x1, waiting for transfers between devices: 3.55 us -> 0.15 us  [body(): lax.all_to_all(jnp.broadcast_to(route[None, :], (n_groups * n_peers, tok_...]
  transfers between devices with their start and end apart: 9 -> 9, of which waited for: 4 -> 4; matrix products, arithmetic and copies ran while one was open for 13% -> 15% of each run, Pallas kernels for 0% -> 0%
where the time goes in v3:
time: 186 us; the launch traced here: 185 us
  waiting for transfers between devices  117 us (63%)
  matrix products  30.4 us (16%)
  starting transfers between devices  18.8 us (10%)
  local copies, waits for them, and re-layouts  9.03 us (5%)
  other arithmetic  8.42 us (5%)
    all_to_all x1, waiting for transfers between devices, step(): lax.all_to_all(packed.reshape(n_peers, block, width), peer_axes, 0, 0, ti...  69.4 us
    all_to_all x1, waiting for transfers between devices, step(): lax.all_to_all(outgoing.reshape(n_peers, block, width), peer_axes, 0, 0,...  44.5 us
    dot_general x13, matrix products, dot(): lax.dot_general(a, b, (dims, ((), ())), preferred_element_type=jnp.float32)  30.4 us
    unnamed x65, local copies, waits for them, and re-layouts  6.77 us
    all_to_all x1, starting transfers between devices, step(): lax.all_to_all(packed.reshape(n_peers, block, width), peer_axes, 0, 0, ti...  6.05 us
    all_to_all x1, starting transfers between devices, body(): lax.all_to_all(jnp.broadcast_to(route[None, :], (n_groups * n_peers, tok_...  5.74 us
    sub x2, other arithmetic, adam_update(): param.astype(jnp.float32) - learn_rate * update  5.31 us
    all_to_all x1, starting transfers between devices, step(): lax.all_to_all(outgoing.reshape(n_peers, block, width), peer_axes, 0, 0,...  4.89 us
  transfers between devices with their start and end apart: 9, of which 4 were waited for; matrix products, arithmetic and copies ran while one was open for 15% of the time, Pallas kernels for 0%

profile of v3, /device:TPU:13, one launch (start us, length us, event | category | flops | bytes accessed | tf_op | source)
XLA Modules:
  0.0 185.4 jit_solution(3884287342346214454)
XLA Ops:
  0.6 0.8 reshape.323
  1.4 0.7 collective-permute-start.7
  2.1 1.3 broadcast_in_dim.82
  3.4 5.7 %all-to-all-start.4 = ((s32[32,1,256]{2,1,0:T(1,128)}), s32[32,1,256]{2,1,0:T(1,128)S(1)}, u32[]{:S(2)}, u32[]{:S(2)}) async-start(s32[32,1,256]{2,1,0:T(1,128)} %broadcast_in_dim.82), calls=%async_computation.4 | async-start | bytes 65536 | tf_op jit(solution)/shard_map/all_to_all | solution.py:57
  9.1 0.4 collective-permute-start.6
  9.6 0.1 collective-permute-start.8
  9.7 0.7 negate_select_fusion.19
  10.4 0.2 fusion.38
  10.6 0.7 fusion.39
  11.3 2.6 %convolution_convert_fusion.3 = bf16[384,4096]{1,0:T(8,128)(2,1)S(1)} fusion(bf16[256,4096]{1,0:T(8,128)(2,1)} %param.13, s32[256]{0:T(256)S(1)} %get-tuple-element.330), kind=kOutput, calls=%fused_computation.108 | convolution fusion | flops 806977536 | bytes 5243904 | tf_op jit(solution)/shard_map/dot_general | solution.py:25
  14.0 0.2 all-to-all-done.4
  14.2 0.2 fusion.52
  14.4 0.6 convert_reduce_fusion
  15.0 0.6 reduce_max.9
  16.4 168.0 %conditional.4 = (f32[4,32]{1,0:T(4,128)S(1)}, f32[4,32,4096]{2,1,0:T(8,128)}, f32[4,32,4096]{2,1,0:T(8,128)}, f32[4,32]{1,0:T(4,128)S(1)}, f32[4,32]{1,0:T(4,12...) conditional(s32[]{:T(128)} %convert_element_type.109, ...), branch_computations={%region_3.7_spmd, %region_7.11_spmd} | conditional | flops 7550543872 | bytes 207238096
  16.7 0.0 copy-start.21
  16.7 0.0 copy-start.36
  16.7 1.6 copy-done.2
  18.3 6.0 %all-to-all-start.2 = ((bf16[16,24,4096]{2,1,0:T(8,128)(2,1)}), bf16[16,24,4096]{2,1,0:T(8,128)(2,1)S(1)}, u32[]{:S(2)}, u32[]{:S(2)}) async-start(bf16[16,24,4096]{2,1,0:T(8,128)(2,1)} %bitcast.123), calls=%async_computation.2 | async-start | bytes 6291456 | tf_op jit(solution)/shard_map/cond/branch_1_fun/all_to_all | solution.py:103
  24.4 0.3 select_reduce_fusion.1
  24.7 0.1 eq.45
  24.8 69.4 %all-to-all-done.2 = bf16[16,24,4096]{2,1,0:T(8,128)(2,1)S(1)} async-done(((bf16[16,24,4096]{2,1,0:T(8,128)(2,1)}), bf16[16,24,4096]{2,1,0:T(8,128)(2,1)S(1)}, u32[]{:S(2)}, u32[]{:S(2)}) %all-to-all-start.2) | async-done | bytes 3145760 | tf_op jit(solution)/shard_map/cond/branch_1_fun/all_to_all | solution.py:103
  94.3 2.3 %convolution_add_fusion.10 = f32[384,128]{1,0:T(8,128)S(1)} fusion(bf16[384,4096]{1,0:T(8,128)(2,1)S(1)} %bitcast.117, bf16[128,4096]{1,0:T(8,128)(2,1)} %get-tuple-element.200, f32[128]{0:T(128)S(1)} %bitcast.146), kind=kOutput, calls=%fused_computation.80 | convolution fusion | flops 402702336 | bytes 4391424 | tf_op jit(solution)/shard_map/cond/branch_1_fun/dot_general | solution.py:25
  96.6 1.7 select_convert_fusion.3
  98.3 4.9 %fusion.74 = (bf16[384,4096]{1,0:T(8,128)(2,1)}, bf16[384,4096]{1,0:T(8,128)(2,1)}) fusion(bf16[16,24,4096]{2,1,0:T(8,128)(2,1)S(1)} %all-to-all-done.2, bf16[128,4096]{1,0:T(8,128)(2,1)} %get-tuple-element.203, bf16[128,4096]{1,0:T(8,128)(2,1)S(1)} %bitcast.129, bf16[384,128]{1,0:T(8,128)(2,1)S(1)} %get-tuple-element.319, ...), kind=kOutput, calls=%fused_computation.186 | convolution fusion | flops 816185344 | bytes 11730944 | tf_op jit(solution)/shard_map/cond/branch_1_fun/dot_general | solution.py:25
  103.2 4.9 %all-to-all-start.3 = ((bf16[16,24,4096]{2,1,0:T(8,128)(2,1)}), bf16[16,24,4096]{2,1,0:T(8,128)(2,1)}, u32[]{:S(2)}, u32[]{:S(2)}) async-start(bf16[16,24,4096]{2,1,0:T(8,128)(2,1)} %bitcast.122), calls=%async_computation.3 | async-start | bytes 6291456 | tf_op jit(solution)/shard_map/cond/branch_1_fun/all_to_all | solution.py:124
  108.0 4.1 %fusion.78 = f32[128,4096]{1,0:T(8,128)} fusion(bf16[384,128]{1,0:T(8,128)(2,1)S(1)} %get-tuple-element.319, bf16[384,4096]{1,0:T(8,128)(2,1)} %get-tuple-element.317), kind=kOutput, calls=%fused_computation.190 | convolution fusion | flops 402653184 | bytes 5341184 | tf_op jit(solution)/shard_map/cond/branch_1_fun/dot_general | solution.py:25
  112.2 0.4 collective-permute-start.5
  112.5 2.3 %fusion.75 = (f32[128]{0:T(128)S(1)}, bf16[384,128]{1,0:T(8,128)(2,1)S(1)}) fusion(bf16[384,4096]{1,0:T(8,128)(2,1)S(1)} %copy-done.1, bf16[128,4096]{1,0:T(8,128)(2,1)} %get-tuple-element.203, s32[128]{0:T(128)S(1)} %broadcast_add_fusion.2, s32[384]{0:T(512)S(1)} %eq.45, f32[384,128]{1,0:T(8,128)S(1)} %convolution_add_fusion.10), kind=kOutput, calls=%fused_computation.187 | convolution fusion | flops 402997120 | bytes 4491776 | tf_op jit(solution)/shard_map/cond/branch_1_fun/dot_general | solution.py:25
  114.8 2.1 %fusion.32 = f32[128,4096]{1,0:T(8,128)} fusion(bf16[384,4096]{1,0:T(8,128)(2,1)S(1)} %bitcast.119, bf16[384,128]{1,0:T(8,128)(2,1)S(1)} %get-tuple-element.322), kind=kOutput, calls=%fused_computation.91 | convolution fusion | flops 402653184 | bytes 5341184 | tf_op jit(solution)/shard_map/cond/branch_1_fun/dot_general | solution.py:25
  116.9 0.1 collective-permute-start.4
  117.0 0.4 collective-permute-start.3
  117.4 1.0 fusion.76
  118.4 2.4 %collective-permute-done.3 = f32[1,128]{1,0:T(1,128)S(1)} collective-permute-done((f32[1,128]{1,0:T(1,128)S(1)}, f32[1,128]{1,0:T(1,128)S(1)}, u32[]{:S(2)}, u32[]{:S(2)}) %collective-permute-start.3) | collective-permute-done | bytes 544 | tf_op jit(solution)/shard_map/cond/branch_1_fun/ppermute | solution.py:139
  120.8 0.1 reshape.314
  120.9 0.6 multiply_subtract_fusion.5
  121.5 3.4 %convolution_add_fusion.6 = f32[128,4096]{1,0:T(8,128)S(1)} fusion(f32[128,4096]{1,0:T(8,128)} %collective-permute-done.5, bf16[384,128]{1,0:T(8,128)(2,1)S(1)} %get-tuple-element.318, bf16[384,4096]{1,0:T(8,128)(2,1)} %get-tuple-element.317), kind=kOutput, calls=%fused_computation.62 | convolution fusion | flops 403177472 | bytes 7438336 | tf_op jit(solution)/shard_map/cond/branch_1_fun/dot_general | solution.py:25
  125.0 0.0 copy-start.6
  125.0 0.0 copy-start.12
  125.0 2.5 %convolution_add_fusion.7 = f32[128,4096]{1,0:T(8,128)S(1)} fusion(f32[128,4096]{1,0:T(8,128)} %collective-permute-done.4, bf16[384,4096]{1,0:T(8,128)(2,1)S(1)} %bitcast.120, bf16[384,128]{1,0:T(8,128)(2,1)S(1)} %get-tuple-element.324), kind=kOutput, calls=%fused_computation.63 | convolution fusion | flops 403177472 | bytes 7438336 | tf_op jit(solution)/shard_map/cond/branch_1_fun/dot_general | solution.py:25
  127.6 0.6 copy-done.10
  128.2 0.6 copy-done.12
  128.8 4.7 %multiply_subtract_fusion.3 = (bf16[4,32,4096]{2,1,0:T(8,128)(2,1)S(1)}, f32[4,32,4096]{2,1,0:T(8,128)}, f32[4,32,4096]{2,1,0:T(8,128)}, bf16[4,32,4096]{2,1,0:T...) fusion(bf16[4,32,4096]{2,1,0:T(8,128)(2,1)S(1)} %copy-done.6, f32[4,32,4096]{2,1,0:T(8,128)S(1)} %bitcast.132, ...), kind=kLoop, calls=%fused_computation.72 | loop fusion | flops 14680064 | bytes 25165824 | tf_op jit(solution)/shard_map/cond/branch_1_fun/sub | solution.py:21
  133.5 44.5 %all-to-all-done.3 = bf16[16,24,4096]{2,1,0:T(8,128)(2,1)} async-done(((bf16[16,24,4096]{2,1,0:T(8,128)(2,1)}), bf16[16,24,4096]{2,1,0:T(8,128)(2,1)}, u32[]{:S(2)}, u32[]{:S(2)}) %all-to-all-start.3) | async-done | bytes 3145760 | tf_op jit(solution)/shard_map/cond/branch_1_fun/all_to_all | solution.py:124
  178.0 3.2 %fusion.20 = bf16[256,4096]{0,1:T(8,128)(2,1)S(1)} fusion(bf16[384,4096]{1,0:T(8,128)(2,1)} %bitcast.19, bf16[384,256]{1,0:T(8,128)(2,1)S(1)} %copy-done.19), kind=kOutput, calls=%fused_computation.61 | convolution fusion | flops 806354944 | bytes 5439488 | tf_op jit(solution)/shard_map/cond/branch_1_fun/dot_general | solution.py:25
  181.2 0.0 copy-start.30
  181.3 2.9 %copy.23 = bf16[256,4096]{1,0:T(8,128)(2,1)} copy(bf16[256,4096]{0,1:T(8,128)(2,1)S(1)} %fusion.20) | data formatting | bytes 4194304
  184.5 0.9 copy-done.18
  (73 shorter events, 0.3 us)
Async XLA Ops:
  1.4 14.9 %collective-permute-start.7 = (f32[1,128]{1,0:T(1,128)S(1)}, f32[1,128]{1,0:T(1,128)S(1)}, u32[]{:S(2)}, u32[]{:S(2)}) collective-permute-start(f32[1,128]{1,0:T(1,128)S(1)} %reshape.323), channel_id=1, source_target_pairs={{0,1},{1,0},{2,3},{3,2},{4,5},{5,4},{6,7},{7,6},{8,9},{9,8},{10,11... | collective-permute-start | bytes 1544 | tf_op jit(solution)/shard_map/ppermute | solution.py:68
  3.4 10.8 %all-to-all-start.4 = ((s32[32,1,256]{2,1,0:T(1,128)}), s32[32,1,256]{2,1,0:T(1,128)S(1)}, u32[]{:S(2)}, u32[]{:S(2)}) async-start(s32[32,1,256]{2,1,0:T(1,128)} %broadcast_in_dim.82), calls=%async_computation.4 | async-start | bytes 65536 | tf_op jit(solution)/shard_map/all_to_all | solution.py:57
  9.1 7.2 %collective-permute-start.6 = (bf16[128,4096]{1,0:T(8,128)(2,1)}, bf16[128,4096]{1,0:T(8,128)(2,1)}, u32[]{:S(2)}, u32[]{:S(2)}) collective-permute-start(bf16[128,4096]{1,0:T(8,128)(2,1)} %bitcast.136), channel_id=1, source_target_pairs={{0,1},{1,0},{2,3},{3,2},{4,5},{5,4},{6,7},{7,6},{8,9},{9,8},{10,11... | collective-permute-start | bytes 3145736 | tf_op jit(solution)/shard_map/ppermute | solution.py:65
  9.6 6.8 %collective-permute-start.8 = (bf16[128,4096]{1,0:T(8,128)(2,1)}, bf16[128,4096]{1,0:T(8,128)(2,1)}, u32[]{:S(2)}, u32[]{:S(2)}) collective-permute-start(bf16[128,4096]{1,0:T(8,128)(2,1)} %bitcast.124), channel_id=1, source_target_pairs={{0,1},{1,0},{2,3},{3,2},{4,5},{5,4},{6,7},{7,6},{8,9},{9,8},{10,11... | collective-permute-start | bytes 3145736 | tf_op jit(solution)/shard_map/ppermute | solution.py:66
  11.3 2.6 %copy-start.23 = (s32[256,1]{0,1:T(1,128)S(1)}, s32[256,1]{0,1:T(1,128)}, u32[]{:S(2)}) copy-start(s32[256,1]{0,1:T(1,128)} %param.14) | copy-start | bytes 3076
  11.3 5.1 %copy-start.20 = (f32[4,32]{1,0:T(4,128)S(1)}, f32[4,32]{1,0:T(4,128)}, u32[]{:S(2)}) copy-start(f32[4,32]{1,0:T(4,128)} %param.16) | copy-start | bytes 1540
  11.3 5.1 %copy-start.24 = (f32[4,32]{1,0:T(4,128)S(1)}, f32[4,32]{1,0:T(4,128)}, u32[]{:S(2)}) copy-start(f32[4,32]{1,0:T(4,128)} %param.20) | copy-start | bytes 1540
  11.3 5.1 %copy-start.27 = (f32[4,32]{1,0:T(4,128)S(1)}, f32[4,32]{1,0:T(4,128)}, u32[]{:S(2)}) copy-start(f32[4,32]{1,0:T(4,128)} %param.21) | copy-start | bytes 1540
  16.7 1.6 copy-start.2
  16.7 1.6 copy-start.21
  16.7 1.6 copy-start.25
  16.7 1.6 copy-start.28
  16.7 1.6 copy-start.36
  18.3 76.0 %all-to-all-start.2 = ((bf16[16,24,4096]{2,1,0:T(8,128)(2,1)}), bf16[16,24,4096]{2,1,0:T(8,128)(2,1)S(1)}, u32[]{:S(2)}, u32[]{:S(2)}) async-start(bf16[16,24,4096]{2,1,0:T(8,128)(2,1)} %bitcast.123), calls=%async_computation.2 | async-start | bytes 6291456 | tf_op jit(solution)/shard_map/cond/branch_1_fun/all_to_all | solution.py:103
  94.3 2.3 %copy-start.16 = (bf16[4,32,4096]{2,1,0:T(8,128)(2,1)S(1)}, bf16[4,32,4096]{2,1,0:T(8,128)(2,1)}, u32[]{:S(2)}) copy-start(bf16[4,32,4096]{2,1,0:T(8,128)(2,1)} %get-tuple-element.210) | copy-start | bytes 3145732
  94.3 2.3 %copy-start.37 = (f32[1,128]{1,0:T(1,128)S(1)}, f32[1,128]{1,0:T(1,128)}, u32[]{:S(2)}) copy-start(f32[1,128]{1,0:T(1,128)} %copy-done.36) | copy-start | bytes 1540
  96.6 1.7 copy-start.4
  103.2 74.9 %all-to-all-start.3 = ((bf16[16,24,4096]{2,1,0:T(8,128)(2,1)}), bf16[16,24,4096]{2,1,0:T(8,128)(2,1)}, u32[]{:S(2)}, u32[]{:S(2)}) async-start(bf16[16,24,4096]{2,1,0:T(8,128)(2,1)} %bitcast.122), calls=%async_computation.3 | async-start | bytes 6291456 | tf_op jit(solution)/shard_map/cond/branch_1_fun/all_to_all | solution.py:124
  108.0 4.5 %copy-start.1 = (bf16[384,4096]{1,0:T(8,128)(2,1)S(1)}, bf16[384,4096]{1,0:T(8,128)(2,1)}, u32[]{:S(2)}) copy-start(bf16[384,4096]{1,0:T(8,128)(2,1)} %get-tuple-element.317) | copy-start | bytes 9437188
  112.2 9.4 %collective-permute-start.5 = (f32[128,4096]{1,0:T(8,128)}, f32[128,4096]{1,0:T(8,128)}, u32[]{:S(2)}, u32[]{:S(2)}) collective-permute-start(f32[128,4096]{1,0:T(8,128)} %fusion.78), channel_id=1, source_target_pairs={{0,1},{1,0},{2,3},{3,2},{4,5},{5,4},{6,7},{7,6},{8,9},{9,8},{10,11... | collective-permute-start | bytes 6291464 | tf_op jit(solution)/shard_map/cond/branch_1_fun/ppermute | solution.py:139
  114.8 2.6 %copy-start.5 = (bf16[4,32,4096]{2,1,0:T(8,128)(2,1)S(1)}, bf16[4,32,4096]{2,1,0:T(8,128)(2,1)}, u32[]{:S(2)}) copy-start(bf16[4,32,4096]{2,1,0:T(8,128)(2,1)} %get-tuple-element.211) | copy-start | bytes 3145732
  114.8 2.6 %copy-start.38 = (f32[384,128]{1,0:T(8,128)S(1)}, f32[384,128]{1,0:T(8,128)}, u32[]{:S(2)}) copy-start(f32[384,128]{1,0:T(8,128)} %get-tuple-element.320) | copy-start | bytes 589828
  116.9 8.1 %collective-permute-start.4 = (f32[128,4096]{1,0:T(8,128)}, f32[128,4096]{1,0:T(8,128)}, u32[]{:S(2)}, u32[]{:S(2)}) collective-permute-start(f32[128,4096]{1,0:T(8,128)} %fusion.32), channel_id=1, source_target_pairs={{0,1},{1,0},{2,3},{3,2},{4,5},{5,4},{6,7},{7,6},{8,9},{9,8},{10,11... | collective-permute-start | bytes 6291464 | tf_op jit(solution)/shard_map/cond/branch_1_fun/ppermute | solution.py:139
  117.0 3.8 %collective-permute-start.3 = (f32[1,128]{1,0:T(1,128)S(1)}, f32[1,128]{1,0:T(1,128)S(1)}, u32[]{:S(2)}, u32[]{:S(2)}) collective-permute-start(f32[1,128]{1,0:T(1,128)S(1)} %bitcast.150), channel_id=1, source_target_pairs={{0,1},{1,0},{2,3},{3,2},{4,5},{5,4},{6,7},{7,6},{8,9},{9,8},{10,11... | collective-permute-start | bytes 1544 | tf_op jit(solution)/shard_map/cond/branch_1_fun/ppermute | solution.py:139
  117.4 3.5 %copy-start.22 = (f32[4,32]{1,0:T(4,128)S(1)}, f32[4,32]{1,0:T(4,128)}, u32[]{:S(2)}) copy-start(f32[4,32]{1,0:T(4,128)} %copy-done.21) | copy-start | bytes 1540
  117.4 3.5 %copy-start.26 = (f32[4,32]{1,0:T(4,128)S(1)}, f32[4,32]{1,0:T(4,128)}, u32[]{:S(2)}) copy-start(f32[4,32]{1,0:T(4,128)} %copy-done.25) | copy-start | bytes 1540
  117.4 3.5 %copy-start.29 = (f32[4,32]{1,0:T(4,128)S(1)}, f32[4,32]{1,0:T(4,128)}, u32[]{:S(2)}) copy-start(f32[4,32]{1,0:T(4,128)} %copy-done.28) | copy-start | bytes 1540
  121.5 6.0 %copy-start.14 = (f32[4,32,4096]{2,1,0:T(8,128)S(1)}, f32[4,32,4096]{2,1,0:T(8,128)}, u32[]{:S(2)}) copy-start(f32[4,32,4096]{2,1,0:T(8,128)} %get-tuple-element.208) | copy-start | bytes 6291460
  121.5 6.0 %copy-start.17 = (bf16[4,32,4096]{2,1,0:T(8,128)(2,1)S(1)}, bf16[4,32,4096]{2,1,0:T(8,128)(2,1)}, u32[]{:S(2)}) copy-start(bf16[4,32,4096]{2,1,0:T(8,128)(2,1)} %get-tuple-element.210) | copy-start | bytes 3145732
  125.0 2.6 %copy-start.6 = (bf16[4,32,4096]{2,1,0:T(8,128)(2,1)S(1)}, bf16[4,32,4096]{2,1,0:T(8,128)(2,1)}, u32[]{:S(2)}) copy-start(bf16[4,32,4096]{2,1,0:T(8,128)(2,1)} %get-tuple-element.211) | copy-start | bytes 3145732
  125.0 2.6 %copy-start.8 = (f32[4,32,4096]{2,1,0:T(8,128)S(1)}, f32[4,32,4096]{2,1,0:T(8,128)}, u32[]{:S(2)}) copy-start(f32[4,32,4096]{2,1,0:T(8,128)} %get-tuple-element.205) | copy-start | bytes 6291460
  125.0 3.2 %copy-start.10 = (f32[4,32,4096]{2,1,0:T(8,128)S(1)}, f32[4,32,4096]{2,1,0:T(8,128)}, u32[]{:S(2)}) copy-start(f32[4,32,4096]{2,1,0:T(8,128)} %get-tuple-element.206) | copy-start | bytes 6291460
  125.0 3.8 %copy-start.12 = (f32[4,32,4096]{2,1,0:T(8,128)S(1)}, f32[4,32,4096]{2,1,0:T(8,128)}, u32[]{:S(2)}) copy-start(f32[4,32,4096]{2,1,0:T(8,128)} %get-tuple-element.207) | copy-start | bytes 6291460
  128.8 49.2 %copy-start.19 = (bf16[384,256]{1,0:T(8,128)(2,1)S(1)}, bf16[384,256]{1,0:T(8,128)(2,1)}, u32[]{:S(2)}) copy-start(bf16[384,256]{1,0:T(8,128)(2,1)} %get-tuple-element.209) | copy-start | bytes 589828
  181.2 2.9 %copy-start.30 = (f32[4,32]{1,0:T(4,128)S(1)}, f32[4,32]{1,0:T(4,128)}, u32[]{:S(2)}) copy-start(f32[4,32]{1,0:T(4,128)} %get-tuple-element.355) | copy-start | bytes 1540
  181.2 2.9 %copy-start.32 = (f32[4,32]{1,0:T(4,128)S(1)}, f32[4,32]{1,0:T(4,128)}, u32[]{:S(2)}) copy-start(f32[4,32]{1,0:T(4,128)} %get-tuple-element.359) | copy-start | bytes 1540
  181.3 2.9 %copy-start.34 = (f32[4,32]{1,0:T(4,128)S(1)}, f32[4,32]{1,0:T(4,128)}, u32[]{:S(2)}) copy-start(f32[4,32]{1,0:T(4,128)} %get-tuple-element.358) | copy-start | bytes 1540
  184.4 1.0 copy-start.18
  184.4 1.0 copy-start.31
  184.5 1.0 copy-start.33
  184.5 0.9 copy-start.35
